TPU v7x, 512 devices: a whole 4x8x8 slice. The times are simulated.
512 devices in a mesh: front: 8 (over x, y_hi), row: 8 (over z), col: 8 (over y_lo, core).
Axes of the slice: x: 4, y: 8 (y_hi: 2, y_lo: 4; y = y_hi * 4 + y_lo), z: 8, core: 2. Of those that a mesh axis runs over, the one named last changes fastest.
Arguments:
- parent_front: bfloat16 [8, 8192, 4096], P('front', 'row', 'col'), may hold values from -3 to 28, as said below
- child_front: bfloat16 [8, 4096, 4096], P('front', 'row', 'col'), may hold values from -2 to 2, as said below
- child_blocks: int32 [8, 16], replicated, may hold values from 0 to 31, as said below
- child_mask: int32 [8, 16, 16], replicated, may hold values from 0 to 1, as said below
Outputs:
- factored_front: float32 [8, 8192, 4096], P('front', 'row', 'col')
Inputs may be any that keep to these rules, and one draw needn't show every extreme that they name: `parent_front`: each parent's matrix is symmetric, and its sum with the extend-add of its two children's masked contributions is positive definite. `child_front`: each child's contribution is symmetric. `child_blocks`: for child c, the tiles a with a % 8 == r map to distinct parent tiles congruent to r modulo 8 that rise with a, and one of them is the last such parent tile. `child_mask`: symmetric in its last two dimensions, with ones on the diagonal.
All inputs are finite; a program needn't handle non-finite values.
Results may differ from a plain program's by a relative error of at most 0.0003.
Values may be sent and summed in bfloat16 or wider, within the bound.
No kernel may reach another device: no remote copies, remote signals or barrier semaphores. Data moves between devices by JAX's collectives and lax.ppermute only.
A program may use at most 64 MiB of HBM per device.

v0:
```python
import jax
import jax.numpy as jnp
from jax import lax
from jax.sharding import PartitionSpec as P

B = 256
PANELS = 2


def broadcast(block, axis, owner):
    block = jnp.where(lax.axis_index(axis) == owner, block, jnp.zeros_like(block))
    return lax.psum(block, axis)


def partner(block, axis, stride):
    count = lax.axis_size(axis)
    route = []
    for low in range(count):
        high = low | 1 << stride
        if high != low and high < count:
            route += [(low, high), (high, low)]
    return lax.ppermute(block, axis, route)


def extend_child(
    update,
    child_index,
    child_blocks,
    child_mask,
    grid_row,
    grid_col,
    half_index,
    row_slots,
    col_slots,
):
    row_count = lax.axis_size("row")
    col_count = lax.axis_size("col")
    crow_slots = update.shape[0] // B
    ccol_slots = update.shape[1] // B
    block_map = lax.dynamic_index_in_dim(child_blocks, child_index, 0, keepdims=False)
    tile_mask = lax.dynamic_index_in_dim(child_mask, child_index, 0, keepdims=False)
    map_down = lax.dynamic_index_in_dim(
        block_map.reshape(crow_slots, row_count), grid_row, 1, keepdims=False
    )
    map_across = lax.dynamic_index_in_dim(
        block_map.reshape(ccol_slots, col_count), grid_col, 1, keepdims=False
    )
    mask_band = lax.dynamic_index_in_dim(
        tile_mask.reshape(crow_slots, row_count, tile_mask.shape[1]), grid_row, 1, keepdims=False
    )
    mask_local = lax.dynamic_index_in_dim(
        mask_band.reshape(crow_slots, ccol_slots, col_count), grid_col, 2, keepdims=False
    )
    row_place = (map_down[None, :] // row_count == jnp.arange(row_slots)[:, None]).astype(
        jnp.bfloat16
    )
    col_match = (map_across[None, :] // (2 * col_count) == jnp.arange(col_slots)[:, None]) & (
        (map_across[None, :] // col_count + map_across[None, :]) % 2 == half_index
    )
    col_place = col_match.astype(jnp.bfloat16)
    tile_values = (
        update.reshape(crow_slots, B, ccol_slots, B)
        * mask_local.astype(jnp.bfloat16)[:, None, :, None]
    )
    placed = jnp.einsum(
        "xa,aibj,yb->xiyj", row_place, tile_values, col_place, preferred_element_type=jnp.float32
    )
    return placed.reshape(row_slots * B, col_slots * B)


def factor_column(column, step_index, grid_row, row_count, row_slots):
    first_row = step_index // row_count * B
    pivot_tile = broadcast(column[first_row : first_row + B], "row", step_index % row_count)
    pivot_factor = jnp.linalg.cholesky(pivot_tile)
    solved = lax.linalg.triangular_solve(
        pivot_factor, column, left_side=False, lower=True, transpose_a=True
    )
    block_global = jnp.arange(row_slots) * row_count + grid_row
    shaped = solved.reshape(row_slots, B, B)
    shaped = jnp.where(
        (block_global > step_index)[:, None, None],
        shaped,
        jnp.where((block_global == step_index)[:, None, None], pivot_factor[None], 0.0),
    )
    return shaped.reshape(row_slots * B, B)


def spread_rows(own_rows, step_index, half_index, col_count):
    owner_half = (step_index // col_count + step_index) % 2
    owner_col = step_index % col_count
    along_cols = broadcast(own_rows, "col", owner_col)
    across = partner(along_cols, "front", 0)
    return jnp.where(half_index == owner_half, along_cols, across)


def column_side(row_panel, half_index, grid_col, row_count, col_count, row_slots, col_slots):
    upper_half = (half_index + grid_col) % 2
    root_row = (upper_half * col_count + grid_col) % row_count
    wanted = (
        jnp.arange(col_slots) * (2 * col_count) + upper_half * col_count + grid_col
    ) // row_count
    selector = (wanted[:, None] == jnp.arange(row_slots)[None, :]).astype(jnp.float32)
    chosen = jnp.einsum(
        "ut,tij->uij", selector, row_panel.reshape(row_slots, B, B), precision=lax.Precision.HIGHEST
    )
    return broadcast(chosen.reshape(col_slots * B, B), "row", root_row)


def trailing(slab, row_panel, col_panel, step_index, row_global, col_global):
    product = lax.dot_general(
        row_panel,
        col_panel,
        (((1,), (1,)), ((), ())),
        precision=lax.Precision.HIGHEST,
        preferred_element_type=jnp.float32,
    )
    slot_count = col_global.shape[0]
    slab_blocks = slab.reshape(slab.shape[0], slot_count, B)
    product_blocks = product.reshape(slab.shape[0], slot_count, B)
    row_later = jnp.repeat(row_global > step_index, B)[:, None, None]
    col_later = (col_global > step_index)[None, :, None]
    col_now = (col_global == step_index)[None, :, None]
    merged = jnp.where(
        col_later,
        jnp.where(row_later, slab_blocks - product_blocks, 0.0),
        jnp.where(col_now, row_panel[:, None, :], slab_blocks),
    )
    return merged.reshape(slab.shape)


def on_device(parent_front, child_front, child_blocks, child_mask):
    row_count = lax.axis_size("row")
    col_count = lax.axis_size("col")
    group_index = lax.axis_index("front")
    grid_row = lax.axis_index("row")
    grid_col = lax.axis_index("col")
    half_index = group_index % 2
    sibling = group_index + 1 - 2 * half_index
    local_front = parent_front[0].astype(jnp.float32)
    row_slots = local_front.shape[0] // B
    col_slots = local_front.shape[1] // B
    own_child = child_front[0]
    other_child = partner(own_child, "front", 0)
    local_front = local_front + extend_child(
        own_child,
        group_index,
        child_blocks,
        child_mask,
        grid_row,
        grid_col,
        half_index,
        row_slots,
        col_slots,
    )
    local_front = local_front + extend_child(
        other_child,
        sibling,
        child_blocks,
        child_mask,
        grid_row,
        grid_col,
        half_index,
        row_slots,
        col_slots,
    )
    row_global = jnp.arange(row_slots) * row_count + grid_row
    col_global = (
        jnp.arange(col_slots) * (2 * col_count) + (half_index + grid_col) % 2 * col_count + grid_col
    )
    for step_index in range(PANELS):
        slot_index = step_index // (2 * col_count)
        own_rows = factor_column(
            local_front[:, slot_index * B : (slot_index + 1) * B],
            step_index,
            grid_row,
            row_count,
            row_slots,
        )
        row_panel = spread_rows(own_rows, step_index, half_index, col_count)
        col_panel = column_side(
            row_panel, half_index, grid_col, row_count, col_count, row_slots, col_slots
        )
        local_front = trailing(
            local_front, row_panel, col_panel, step_index, row_global, col_global
        )
    return local_front[None]


def solution(mesh):
    return jax.shard_map(
        on_device,
        mesh=mesh,
        in_specs=(P("front", "row", "col"), P("front", "row", "col"), P(), P()),
        out_specs=P("front", "row", "col"),
        check_vma=False,
    )
```

profile of v0, /device:TPU:6, one launch (start us, length us, event | category | flops | bytes accessed | tf_op | source)
XLA Modules:
  0.0 817.8 jit_solution(14027624428790879510)
XLA Ops:
  6.5 7.7 collective-permute-start
  14.3 1.2 reshape_squeeze.3
  19.5 2.3 convolution_bitcast_fusion.1
  22.6 3.2 copy.21
  25.9 1.8 copy.45
  28.0 9.0 %collective-permute-done = bf16[512,512]{1,0:T(8,128)(2,1)} collective-permute-done((bf16[512,512]{1,0:T(8,128)(2,1)}, bf16[512,512]{1,0:T(8,128)(2,1)}, u32[]{:S(2)}, u32[]{:S(2)}) %collective-permute-start) | collective-permute-done | bytes 524320 | tf_op jit(solution)/shard_map/ppermute | solution.py:22
  37.0 2.0 reshape.576
  39.0 1.8 fusion.17
  40.8 2.3 convolution_bitcast_fusion
  43.1 4.1 copy.22
  47.3 2.2 copy.46
  50.3 1.3 copy-done.1
  52.7 83.7 %all-reduce.8.cloned.1.call-done = f32[256,256]{0,1:T(8,128)} async-done(((f32[256,256]{0,1:T(8,128)}), f32[256,256]{0,1:T(8,128)}) %all-reduce.8.cloned.1.call-update) | async-done | bytes 262160 | tf_op jit(solution)/shard_map/psum | solution.py:12
  136.4 1.1 copy.25
  137.5 1.0 fusion.22
  138.5 11.7 %cholesky.130 = f32[128,128]{1,0:T(8,128)S(1)} custom-call(f32[128,128]{1,0:T(8,128)S(1)} %cholesky.194), custom_call_target="Cholesky" | custom-call | tf_op jit(solution)/shard_map/jit(cholesky)/cholesky | solution.py:74
  150.9 9.8 %custom-call.13 = f32[1,128,128]{1,2,0:T(8,128)S(1)} custom-call(f32[1,128,128]{2,1,0:T(8,128)S(1)} %get-tuple-element.62), custom_call_target="InvertDiagBlocksLowerTriangular" | custom-call | tf_op jit(solution)/shard_map/jit(cholesky)/cholesky | solution.py:74
  161.2 11.7 %cholesky.147 = f32[128,128]{1,0:T(8,128)S(1)} custom-call(f32[128,128]{1,0:T(8,128)S(1)} %convolution_subtract_fusion.2), custom_call_target="Cholesky" | custom-call | tf_op jit(solution)/shard_map/jit(cholesky)/cholesky | solution.py:74
  175.1 4.2 while.4
  176.0 1.4 bitcast_dynamic-update-slice_fusion.4
  177.9 1.4 bitcast_dynamic-update-slice_fusion.4
  179.9 19.7 %custom-call.14 = f32[2,128,128]{1,2,0:T(8,128)S(1)} custom-call(f32[2,128,128]{2,1,0:T(8,128)S(1)} %get-tuple-element.21), custom_call_target="InvertDiagBlocksLowerTriangular" | custom-call | tf_op jit(solution)/shard_map/triangular_solve/custom-call.0 | solution.py:75
  199.5 1.7 fusion.15
  201.2 1.7 convolution_subtract_fusion
  203.9 1.2 fusion.8
  205.2 77.4 %all-reduce.10.cloned.1.call-done = f32[1024,256]{0,1:T(8,128)} async-done(((f32[1024,256]{0,1:T(8,128)}), f32[1024,256]{0,1:T(8,128)}) %all-reduce.10.cloned.1.call-update) | async-done | bytes 1048592 | tf_op jit(solution)/shard_map/psum | solution.py:12
  282.6 5.5 collective-permute-start.1
  288.1 46.0 %collective-permute-done.1 = f32[1024,256]{0,1:T(8,128)} collective-permute-done((f32[1024,256]{0,1:T(8,128)}, f32[1024,256]{0,1:T(8,128)}, u32[]{:S(2)}, u32[]{:S(2)}) %collective-permute-start.1) | collective-permute-done | bytes 1048608 | tf_op jit(solution)/shard_map/ppermute | solution.py:22
  334.2 1.4 broadcast_select_fusion.1
  335.5 1.5 reshape.582
  337.0 2.3 copy.27
  339.3 2.3 convolution_select_fusion.1
  342.7 79.2 %all-reduce.12.cloned.1.call-done = f32[512,256]{1,0:T(8,128)} async-done(((f32[512,256]{1,0:T(8,128)}), f32[512,256]{1,0:T(8,128)}) %all-reduce.12.cloned.1.call-update) | async-done | bytes 524304 | tf_op jit(solution)/shard_map/psum | solution.py:12
  421.9 5.3 fusion.5
  427.3 1.3 copy-done.5
  429.9 76.2 %all-reduce.14.cloned.1.call-done = f32[256,256]{0,1:T(8,128)} async-done(((f32[256,256]{0,1:T(8,128)}), f32[256,256]{0,1:T(8,128)}) %all-reduce.14.cloned.1.call-update) | async-done | bytes 262160 | tf_op jit(solution)/shard_map/psum | solution.py:12
  506.1 1.1 copy.31
  507.2 1.0 fusion.21
  508.9 11.7 %cholesky.164 = f32[128,128]{1,0:T(8,128)S(1)} custom-call(f32[128,128]{1,0:T(8,128)S(1)} %cholesky.197), custom_call_target="Cholesky" | custom-call | tf_op jit(solution)/shard_map/jit(cholesky)/cholesky | solution.py:74
  521.3 9.8 %custom-call.15 = f32[1,128,128]{1,2,0:T(8,128)S(1)} custom-call(f32[1,128,128]{2,1,0:T(8,128)S(1)} %get-tuple-element.58), custom_call_target="InvertDiagBlocksLowerTriangular" | custom-call | tf_op jit(solution)/shard_map/jit(cholesky)/cholesky | solution.py:74
  531.1 1.0 constant_dynamic-update-slice_fusion
  532.2 1.1 convolution_subtract_fusion.1
  533.3 11.7 %cholesky.181 = f32[128,128]{1,0:T(8,128)S(1)} custom-call(f32[128,128]{1,0:T(8,128)S(1)} %convolution_subtract_fusion.1), custom_call_target="Cholesky" | custom-call | tf_op jit(solution)/shard_map/jit(cholesky)/cholesky | solution.py:74
  547.8 1.8 copy.32
  549.6 5.4 while.5
  551.0 1.4 bitcast_dynamic-update-slice_fusion.5
  553.6 1.4 bitcast_dynamic-update-slice_fusion.5
  555.6 20.5 %custom-call.16 = f32[2,128,128]{1,2,0:T(8,128)S(1)} custom-call(f32[2,128,128]{2,1,0:T(8,128)} %copy-done.10), custom_call_target="InvertDiagBlocksLowerTriangular" | custom-call | tf_op jit(solution)/shard_map/triangular_solve/custom-call.0 | solution.py:75
  576.1 1.7 fusion.13
  578.5 1.7 fusion.12
  580.6 1.2 fusion.9
  581.8 77.3 %all-reduce.16.cloned.1.call-done = f32[1024,256]{0,1:T(8,128)} async-done(((f32[1024,256]{0,1:T(8,128)}), f32[1024,256]{0,1:T(8,128)}) %all-reduce.16.cloned.1.call-update) | async-done | bytes 1048592 | tf_op jit(solution)/shard_map/psum | solution.py:12
  659.2 5.5 collective-permute-start.2
  664.7 46.1 %collective-permute-done.2 = f32[1024,256]{0,1:T(8,128)} collective-permute-done((f32[1024,256]{0,1:T(8,128)}, f32[1024,256]{0,1:T(8,128)}, u32[]{:S(2)}, u32[]{:S(2)}) %collective-permute-start.2) | collective-permute-done | bytes 1048608 | tf_op jit(solution)/shard_map/ppermute | solution.py:22
  710.7 2.4 broadcast_select_fusion
  713.1 2.7 reshape.584
  715.8 2.3 copy.33
  718.1 2.3 convolution_select_fusion
  720.4 0.9 copy.34
  721.4 2.1 reshape.574
  723.7 3.5 reshape.579
  727.2 73.7 %all-reduce.18.cloned.1.call-done = f32[512,256]{1,0:T(8,128)} async-done(((f32[512,256]{1,0:T(8,128)}), f32[512,256]{1,0:T(8,128)}) %all-reduce.18.cloned.1.call-update) | async-done | bytes 524304 | tf_op jit(solution)/shard_map/psum | solution.py:12
  800.8 7.0 fusion.3
  807.8 2.9 copy.36
  (122 shorter events, 21.7 us)
Async XLA Ops:
  6.5 129.8 %all-reduce.8.cloned.1.call-start = ((), (), s32[]{:S(2)}) async-start(), calls=%async_computation | async-start | bytes 524288 | tf_op jit(solution)/shard_map/psum | solution.py:12
  6.5 30.5 %collective-permute-start = (bf16[512,512]{1,0:T(8,128)(2,1)}, bf16[512,512]{1,0:T(8,128)(2,1)}, u32[]{:S(2)}, u32[]{:S(2)}) collective-permute-start(bf16[512,512]{1,0:T(8,128)(2,1)} %bitcast.175), channel_id=1, source_target_pairs={{0,64},{64,0},{128,192},{192,128},{256,320},{320,256},{384,448},{4... | collective-permute-start | bytes 1572872 | tf_op jit(solution)/shard_map/ppermute | solution.py:22
  19.5 2.5 copy-start.7
  22.6 26.9 %copy-start.2 = (bf16[1,1024,512]{1,2,0:T(8,128)(2,1)}, bf16[1,1024,512]{1,2,0:T(8,128)(2,1)S(1)}, u32[]{:S(2)}) copy-start(bf16[1,1024,512]{1,2,0:T(8,128)(2,1)S(1)} %copy.20) | copy-start | bytes 3145732
  47.3 2.2 copy-start.4
  50.2 1.3 copy-start.1
  52.3 230.3 %all-reduce.10.cloned.1.call-start = ((), (), s32[]{:S(2)}) async-start(), calls=%async_computation.1 | async-start | bytes 2097152 | tf_op jit(solution)/shard_map/psum | solution.py:12
  179.3 0.6 copy-start.17
  205.1 216.8 %all-reduce.12.cloned.1.call-start = ((), (), s32[]{:S(2)}) async-start(), calls=%async_computation.2 | async-start | bytes 1048576 | tf_op jit(solution)/shard_map/psum | solution.py:12
  282.6 51.6 %collective-permute-start.1 = (f32[1024,256]{0,1:T(8,128)}, f32[1024,256]{0,1:T(8,128)}, u32[]{:S(2)}, u32[]{:S(2)}) collective-permute-start(f32[1024,256]{0,1:T(8,128)} %all-reduce.10.cloned.1.call-done), channel_id=1, source_target_pairs={{0,64},{64,0},{128,192},{192,128},{256,320},{320,256},{384,448},{4... | collective-permute-start | bytes 3145736 | tf_op jit(solution)/shard_map/ppermute | solution.py:22
  342.5 163.6 %all-reduce.14.cloned.1.call-start = ((), (), s32[]{:S(2)}) async-start(), calls=%async_computation.3 | async-start | bytes 524288 | tf_op jit(solution)/shard_map/psum | solution.py:12
  342.6 84.6 %copy-start.11 = (pred[512]{0:T(512)(128)(4,1)}, pred[512]{0:T(512)(128)(4,1)S(1)}, u32[]{:S(2)}) copy-start(pred[512]{0:T(512)(128)(4,1)S(1)} %broadcast_in_dim.217) | copy-start | bytes 1540
  342.7 84.5 %copy-start.13 = (pred[512]{0:T(512)(128)(4,1)}, pred[512]{0:T(512)(128)(4,1)S(1)}, u32[]{:S(2)}) copy-start(pred[512]{0:T(512)(128)(4,1)S(1)} %broadcast_in_dim.199) | copy-start | bytes 1540
  427.3 1.3 copy-start.5
  429.3 229.9 %all-reduce.16.cloned.1.call-start = ((), (), s32[]{:S(2)}) async-start(), calls=%async_computation.4 | async-start | bytes 2097152 | tf_op jit(solution)/shard_map/psum | solution.py:12
  508.2 0.7 copy-start.9
  545.0 2.0 copy-start.8
  555.0 0.7 copy-start.10
  576.1 4.0 copy-start.6
  581.8 219.0 %all-reduce.18.cloned.1.call-start = ((), (), s32[]{:S(2)}) async-start(), calls=%async_computation.5 | async-start | bytes 1048576 | tf_op jit(solution)/shard_map/psum | solution.py:12
  659.2 51.6 %collective-permute-start.2 = (f32[1024,256]{0,1:T(8,128)}, f32[1024,256]{0,1:T(8,128)}, u32[]{:S(2)}, u32[]{:S(2)}) collective-permute-start(f32[1024,256]{0,1:T(8,128)} %all-reduce.16.cloned.1.call-done), channel_id=1, source_target_pairs={{0,64},{64,0},{128,192},{192,128},{256,320},{320,256},{384,448},{4... | collective-permute-start | bytes 3145736 | tf_op jit(solution)/shard_map/ppermute | solution.py:22
  721.4 2.1 copy-start.16
  721.4 2.2 copy-start.15
  723.7 77.2 %copy-start = (f32[1024,256]{0,1:T(8,128)S(1)}, f32[1024,256]{0,1:T(8,128)}, u32[]{:S(2)}) copy-start(f32[1024,256]{0,1:T(8,128)} %broadcast_select_fusion) | copy-start | bytes 3145732
  723.7 77.2 %copy-start.3 = (bf16[1,1024,512]{1,2,0:T(8,128)(2,1)S(1)}, bf16[1,1024,512]{1,2,0:T(8,128)(2,1)}, u32[]{:S(2)}) copy-start(bf16[1,1024,512]{1,2,0:T(8,128)(2,1)} %copy-done.2) | copy-start | bytes 3145732
  723.7 77.2 %copy-start.12 = (pred[512]{0:T(512)(128)(4,1)S(1)}, pred[512]{0:T(512)(128)(4,1)}, u32[]{:S(2)}) copy-start(pred[512]{0:T(512)(128)(4,1)} %copy-done.11) | copy-start | bytes 1540
  723.7 77.2 %copy-start.14 = (pred[512]{0:T(512)(128)(4,1)S(1)}, pred[512]{0:T(512)(128)(4,1)}, u32[]{:S(2)}) copy-start(pred[512]{0:T(512)(128)(4,1)} %copy-done.13) | copy-start | bytes 1540
Sparse Core Ops, SparseCore 0:
  52.4 83.9 all-reduce.7
  205.2 77.3 all-reduce.9
  342.6 79.2 all-reduce.11
  429.4 76.6 all-reduce.13
  581.9 77.2 all-reduce.15
  721.5 79.2 all-reduce.17
where the time goes:
time: 824 us; the launch traced here: 818 us
  waiting for transfers between devices  569 us (69%)
  other arithmetic  122 us (15%)
  local copies, waits for them, and re-layouts  55.5 us (7%)
  matrix products  34.8 us (4%)
  starting transfers between devices  19.5 us (2%)
  between operations  16.8 us (2%)
    psum x6, waiting for transfers between devices, broadcast(): return lax.psum(block, axis)  467 us
    ppermute x3, waiting for transfers between devices, partner(): return lax.ppermute(block, axis, route)  101 us
    another operation x14, other arithmetic, factor_column(): pivot_factor = jnp.linalg.cholesky(pivot_tile)  69.3 us
    another operation x5, other arithmetic, factor_column(): lax.linalg.triangular_solve(pivot_factor, column, left_side=False, lower=...  40.9 us
    ppermute x3, starting transfers between devices, partner(): return lax.ppermute(block, axis, route)  18.7 us
  transfers between devices with their start and end apart: 9, of which 9 were waited for; matrix products, arithmetic and copies ran while one was open for 2% of the time, Pallas kernels for 0%

commit v1 on v0

v1 whole, which is shorter than its diff:
```python
import jax
import jax.numpy as jnp
from jax import lax
from jax.experimental import pallas as pl
from jax.experimental.pallas import tpu as pltpu
from jax.sharding import Mesh
from jax.sharding import PartitionSpec as P

B = 256
H = 128
F32 = jnp.float32
BF16 = jnp.bfloat16


def matmul(a, b, dims, precision=lax.Precision.HIGHEST):
    return lax.dot_general(a, b, (dims, ((), ())), precision=precision, preferred_element_type=F32)


NT = ((1,), (1,))
NN = ((1,), (0,))


def split(a):
    high = a.astype(BF16)
    return high, (a - high.astype(F32)).astype(BF16)


def three_pass(a, b, dims):
    (ah, al), (bh, bl) = a, b
    dot = lambda x, y: lax.dot_general(x, y, (dims, ((), ())), preferred_element_type=F32)
    return dot(ah, bh) + (dot(ah, bl) + dot(al, bh))


def inverse_factor(strips):
    sub = lax.broadcasted_iota(jnp.int32, (8, H), 0)
    lane = lax.broadcasted_iota(jnp.int32, (8, H), 1)
    count = H // 8
    body = list(strips)
    inv = [(lane == sub + 8 * s).astype(F32) for s in range(count)]
    row_of = lambda v, j: jnp.broadcast_to(v[j : j + 1, :], (8, H))
    for s in range(count):
        cols = {
            t: [jnp.broadcast_to(body[t][:, 8 * s + j : 8 * s + j + 1], (8, H)) for j in range(8)]
            for t in range(s, count)
        }
        for j in range(8):
            scale = lax.rsqrt(row_of(cols[s][j], j))
            row_body = row_of(body[s], j) * scale
            row_inv = row_of(inv[s], j) * scale
            own = cols[s][j] * scale
            coeff = {m: row_of(own, m) for m in range(j + 1, 8)}
            for t in range(s, count):
                col = own if t == s else cols[t][j] * scale
                for m in range(j + 1, 8):
                    cols[t][m] = cols[t][m] - col * coeff[m]
                if t == s:
                    low = jnp.where(sub > j, col, 0.0)
                    body[t] = body[t] - low * row_body
                    inv[t] = jnp.where(sub == j, row_inv, inv[t] - low * row_inv)
                else:
                    body[t] = body[t] - col * row_body
                    inv[t] = inv[t] - col * row_inv
    return jnp.concatenate(inv, axis=0)


def at(k):
    return slice(k * H, (k + 1) * H)


def factor_tile(work, first):
    inv, low = {}, {}
    last = first + 1
    for b in (first, last):
        inv[b] = inverse_factor(
            [work[b * H + 8 * s : b * H + 8 * s + 8, at(b)] for s in range(H // 8)]
        )
        if b == first:
            low = matmul(work[at(last), at(b)], inv[b], NT)
            work[at(last), at(last)] -= matmul(low, low, NT)
    return inv[first], inv[last], -matmul(inv[last], matmul(low, inv[first], NN), NN)


def store_inverse(x_ref, blocks):
    top, low, corner = blocks
    x_ref[0:H, 0:H] = top
    x_ref[H:, H:] = low
    x_ref[0:H, H:] = jnp.zeros((H, H), F32)
    x_ref[H:, 0:H] = corner


def first_kernel(where, mine_ref, theirs_ref, x0_ref, l10_ref, rest_ref, work):
    even = where[2] == 0
    work[...] = jnp.where(even, mine_ref[0:B], theirs_ref[0:B])
    store_inverse(x0_ref, factor_tile(work, 0))
    d01 = jnp.where(even, theirs_ref[0:B], mine_ref[0:B])
    low = matmul(d01.T, x0_ref[...], NT)
    l10_ref[...] = low
    rest_ref[...] = jnp.where(even, theirs_ref[B:], mine_ref[B:]) - matmul(low, low, NT)


def second_kernel(rest_ref, x1_ref, work):
    work[...] = rest_ref[...]
    store_inverse(x1_ref, factor_tile(work, 0))


TILE = jax.ShapeDtypeStruct((B, B), F32)
VMEM = pl.BlockSpec(memory_space=pltpu.VMEM)
COST = pl.CostEstimate(flops=10**10, bytes_accessed=2**20, transcendentals=0)
PARAMS = pltpu.CompilerParams(vmem_limit_bytes=32 * 2**20)


def first_pivot(where, mine, theirs):
    return pl.pallas_call(
        first_kernel,
        out_shape=(TILE, TILE, TILE),
        in_specs=[pl.BlockSpec(memory_space=pltpu.SMEM), VMEM, VMEM],
        scratch_shapes=[pltpu.VMEM((B, B), F32)],
        compiler_params=PARAMS,
        cost_estimate=COST,
    )(where, mine, theirs)


def second_pivot(rest):
    return pl.pallas_call(
        second_kernel,
        out_shape=TILE,
        in_specs=[VMEM],
        scratch_shapes=[pltpu.VMEM((B, B), F32)],
        compiler_params=PARAMS,
        cost_estimate=COST,
    )(rest)


def final_kernel(
    place, where, parent_ref, own_ref, top_ref, low_ref, mine_ref, theirs_ref, g_ref, h_ref,
    x0_ref, x1_ref, l10_ref, out_ref, across, xs,
):
    slot = pl.program_id(0)

    @pl.when(slot == 0)
    def _():
        for k, ref in enumerate((x0_ref, x1_ref, l10_ref)):
            xs[2 * k], xs[2 * k + 1] = split(ref[...])
        x0, x1, l10 = [(xs[2 * k], xs[2 * k + 1]) for k in range(3)]
        dot = lambda a, b: lax.dot_general(a, b, (NN, ((), ())), preferred_element_type=F32)
        g = g_ref[...]
        q0 = dot(x0[0], g) + dot(x0[1], g)
        q1 = three_pass(x1, split(h_ref[...].astype(F32) - three_pass(l10, split(q0), NN)), NN)
        across[0:B] = q0.astype(BF16)
        across[B:] = q1.astype(BF16)

    x0, x1, l10 = [(xs[2 * k], xs[2 * k + 1]) for k in range(3)]
    even = where[2] == 0
    mine, theirs = mine_ref[...], theirs_ref[...]
    p0 = three_pass(split(jnp.where(even, mine, theirs)), x0, NT)
    p0s = split(p0)
    p1 = three_pass(split(jnp.where(even, theirs, mine) - three_pass(p0s, l10, NT)), x1, NT)
    p1s = split(p1)
    row = where[0] + 8 * slot
    lead = row < 2
    last = (slot == 3).astype(jnp.int32)
    from_row = pl.multiple_of(last * B, B)
    for v in range(2):
        cols = slice(v * B, (v + 1) * B)
        value = parent_ref[:, cols].astype(F32)
        for b in range(v + 1):
            here = slice(b * B, (b + 1) * B)
            sib = jnp.where(last == 1, low_ref[:, here].astype(F32), top_ref[:, here].astype(F32))
            own = own_ref[pl.ds(from_row, B), here].astype(F32)
            for child, part in enumerate((own, sib)):
                w = place[(((child * 2 + last) * 2 + b) * 4 + slot) * 2 + v]
                value += w * part
        q0, q1 = across[0:B, cols], across[B:, cols]
        dot = lambda a, b: lax.dot_general(a, b, (NN, ((), ())), preferred_element_type=F32)
        value -= (dot(p0s[0], q0) + dot(p1s[0], q1)) + (dot(p0s[1], q0) + dot(p1s[1], q1))
        out_ref[:, cols] = jnp.where(lead, 0.0, value)
    tril = lax.broadcasted_iota(jnp.int32, (B, B), 0) >= lax.broadcasted_iota(jnp.int32, (B, B), 1)

    @pl.when(where[1] == 0)
    def _():
        out_ref[:, 0:B] = jnp.where(jnp.logical_or(tril, row > 0), p0, 0.0)

    @pl.when(where[1] == 1)
    def _():
        keep = jnp.logical_and(jnp.logical_or(tril, row > 1), row > 0)
        out_ref[:, 0:B] = jnp.where(keep, p1, 0.0)


def finish(place, where, parent, own, top, low, mine, theirs, g, h, x0, x1, l10):
    whole = lambda shape: pl.BlockSpec(shape, lambda i, *_: (0, 0))
    rows = lambda width: pl.BlockSpec((B, width), lambda i, *_: (i, 0))
    wide, tile = whole((B, 2 * B)), whole((B, B))
    return pl.pallas_call(
        final_kernel,
        out_shape=jax.ShapeDtypeStruct(parent.shape, F32),
        grid_spec=pltpu.PrefetchScalarGridSpec(
            num_scalar_prefetch=2,
            grid=(parent.shape[0] // B,),
            in_specs=[
                rows(2 * B), whole((2 * B, 2 * B)), wide, wide, rows(B), rows(B),
                wide, wide, tile, tile, tile,
            ],
            out_specs=rows(2 * B),
            scratch_shapes=[pltpu.VMEM((2 * B, 2 * B), BF16), pltpu.VMEM((6, B, B), BF16)],
        ),
        compiler_params=pltpu.CompilerParams(vmem_limit_bytes=48 * 2**20),
    )(place, where, parent, own, top, low, mine, theirs, g, h, x0, x1, l10)


def tie(value, *after):
    return lax.optimization_barrier((value, *after))[0]


def one_of(index, places):
    hit = index == places[0]
    for place in places[1:]:
        hit = jnp.logical_or(hit, index == place)
    return hit


class Along:
    def __init__(self, axes, index, first, second, third, fourth, zero, one):
        self.axes, self.index = axes, index
        self.routes = first, second, third, fourth
        self.zero, self.one = zero, one

    def send(self, value, k):
        return lax.ppermute(value, self.axes, self.routes[k])

    def start(self, block):
        first, second = self.send(block, 0), self.send(block, 1)
        ends = lambda k: [dst for _, dst in self.routes[k]]
        return jnp.where(
            one_of(self.index, ends(0)), first, jnp.where(one_of(self.index, ends(1)), second, block)
        )

    def end(self, held):
        third, fourth = self.send(held, 2), self.send(held, 3)
        pick = lambda own, near: jnp.where(
            one_of(self.index, own), held, jnp.where(one_of(self.index, near), third, fourth)
        )
        return pick(*self.zero), pick(*self.one)


def ring_y(y):
    return Along(
        ("y_hi", "y_lo"), y, [(0, 3), (4, 7)], [(0, 5), (4, 1)],
        [(0, 1), (3, 4), (5, 6), (4, 5), (7, 0), (1, 2)], [(0, 7), (3, 2), (4, 3), (7, 6)],
        ((0, 3, 5), (1, 4, 6)), ((4, 7, 1), (5, 0, 2)),
    )


def ring_z(z):
    return Along(
        "row", z, [(0, 5), (1, 4)], [(0, 2), (1, 7)],
        [(0, 1), (5, 4), (2, 3), (1, 2), (4, 5), (7, 6)], [(0, 7), (5, 6), (1, 0), (4, 3)],
        ((0, 2, 5), (1, 3, 4)), ((1, 4, 7), (2, 5, 6)),
    )


def direct_z(block, z, before_last):
    late = tie(block, before_last)
    recv = [
        lax.ppermute(
            block if s < 5 else late, ("row", "core"), [(0, 2 * s), (1, 2 * s + 1), (3, 2 * ((1 + s) % 8) + 1)]
        )
        for s in range(1, 8)
    ]
    zero, one = block, block
    for s in range(1, 8):
        zero = jnp.where(z == s, recv[s - 1], zero)
        one = jnp.where(z == (1 + s) % 8, recv[s - 1], one)
    return jnp.concatenate([zero, one], axis=0), recv[0]


def on_device(parent, child, child_blocks, child_mask):
    parent, child = parent[0], child[0]
    x, half = lax.axis_index("x"), lax.axis_index("y_hi")
    z, y_lo, core = lax.axis_index("row"), lax.axis_index("y_lo"), lax.axis_index("core")
    z = z.astype(jnp.int32)
    y = half * 4 + y_lo
    col = 2 * y_lo + core
    other = lambda value: lax.ppermute(value, "core", [(0, 1), (1, 0)])

    maps = lax.dynamic_slice(child_blocks, (2 * x, 0), (2, 16))
    masks = lax.dynamic_slice(child_mask, (2 * x, 0, 0), (2, 16, 16))
    down = lax.dynamic_index_in_dim(maps.reshape(2, 2, 8), z, 2, keepdims=False)
    over = lax.dynamic_index_in_dim(maps.reshape(2, 2, 8), col, 2, keepdims=False)
    mask_rows = lax.dynamic_index_in_dim(masks.reshape(2, 2, 8, 16), z, 2, keepdims=False)
    mask_here = lax.dynamic_index_in_dim(mask_rows.reshape(2, 2, 2, 8), col, 3, keepdims=False)
    mask_core = lax.dynamic_index_in_dim(mask_rows, core, 2, keepdims=False)
    first_col = (half + y_lo * 2 + core) % 2 * 8 + col
    row_hit = down[:, :, None] == 8 * jnp.arange(4) + z
    col_hit = over[:, :, None] == 16 * jnp.arange(2) + first_col
    place = (
        row_hit[:, :, None, :, None]
        & col_hit[:, None, :, None, :]
        & (mask_here > 0)[:, :, :, None, None]
    ).astype(F32)
    panel_hit = lax.dynamic_index_in_dim(maps, core, 1, keepdims=False) == core
    panel_place = (row_hit & (mask_core > 0)[:, :, None] & panel_hit[:, None, None]).astype(F32)

    place = jnp.where(half == 1, place[::-1], place)
    special = jnp.where(
        jnp.logical_and(half == 0, col == 0), 0, jnp.where(jnp.logical_and(half == 1, col == 1), 1, 2)
    )
    where = jnp.stack([z, special, core]).astype(jnp.int32)
    spread_y, spread_z = ring_y(y), ring_z(z)
    swap = lambda value: lax.ppermute(value, "y_hi", [(0, 1), (1, 0)])

    lead = jnp.concatenate([parent[:B, :B], child[:B, :B]], axis=0)
    held = spread_y.start(lead)
    from0, from4 = spread_y.end(held)
    base = jnp.where(core == 0, from0[:B], from4[:B]).astype(F32)
    childs = [from0[B:].astype(F32), from4[B:].astype(F32)]
    top = base + panel_place[0, 0, 0] * childs[0] + panel_place[1, 0, 0] * childs[1]
    sib_top = swap(tie(child[:B], held))
    pivot_rows, early = direct_z(top, z, sib_top)
    theirs = other(pivot_rows)

    rest = jnp.concatenate([parent[B:, :B], child[B:, :B]], axis=0)
    rest_held = spread_y.start(tie(rest, early))

    strip = parent[:B].astype(F32).reshape(B, 2, B)
    for k, ref in ((0, child[:B]), (1, sib_top)):
        for b in range(2):
            strip += place[k, 0, b, 0][None, :, None] * ref[:, None, b * B : (b + 1) * B].astype(F32)
    strip_held = spread_z.start(tie(strip.reshape(B, 2 * B).astype(BF16), early))
    rest0, rest4 = spread_y.end(tie(rest_held, pivot_rows))

    x0, l10, low = first_pivot(tie(where, strip_held), pivot_rows, theirs)
    g, h = spread_z.end(tie(strip_held, pivot_rows))
    sib_low = swap(tie(child[B:], rest_held))
    tiles = jnp.where(core == 0, rest0[: 3 * B], rest4[: 3 * B]).astype(F32)
    below = [
        tiles[(s - 1) * B : s * B]
        + panel_place[0, s // 3, s] * (rest0[3 * B :].astype(F32) if s == 3 else childs[0])
        + panel_place[1, s // 3, s] * (rest4[3 * B :].astype(F32) if s == 3 else childs[1])
        for s in range(1, 4)
    ]
    column = jnp.concatenate([top, *below], axis=0)
    column_other = other(tie(column, x0))
    x1 = second_pivot(tie(low, column))
    out = finish(
        place.reshape(-1), where, parent, child, sib_top, sib_low, column, column_other,
        g, h, x0, x1, l10,
    )
    return out[None]


def solution(mesh):
    shape = mesh.shape
    if (shape["front"], shape["row"], shape["col"]) != (8, 8, 8):
        raise ValueError("mesh shape")
    fine = Mesh(
        mesh.devices.reshape(4, 2, 8, 4, 2), ("x", "y_hi", "row", "y_lo", "core")
    )
    spec = P(("x", "y_hi"), "row", ("y_lo", "core"))
    return jax.shard_map(
        on_device, mesh=fine, in_specs=(spec, spec, P(), P()), out_specs=spec, check_vma=False
    )
```

time: 824 us -> 146 us (0.18)
  the two profiles are of different devices: /device:TPU:6 before, /device:TPU:39 now
where the time goes in v1:
time: 146 us; the launch traced here: 145 us
  starting transfers between devices  67.5 us (46%)
  waiting for transfers between devices  34.4 us (24%)
  Pallas kernels  27.1 us (19%)
  other arithmetic  9.32 us (6%)
  local copies, waits for them, and re-layouts  6 us (4%)
    ppermute x12, starting transfers between devices, send(): return lax.ppermute(value, self.axes, self.routes[k])  36.6 us
    ppermute x12, waiting for transfers between devices, send(): return lax.ppermute(value, self.axes, self.routes[k])  19.4 us
    ppermute x7, starting transfers between devices, direct_z(): lax.ppermute(block if s < 5 else late, ('row', 'core'), [(0, 2 * s), (1,...  19.3 us
    ppermute x7, waiting for transfers between devices, direct_z(): lax.ppermute(block if s < 5 else late, ('row', 'core'), [(0, 2 * s), (1,...  15 us
    pallas_call x1, Pallas kernels, first_pivot(): pl.pallas_call(first_kernel, out_shape=(TILE, TILE, TILE), in_specs=[pl.B...  10.5 us
    pallas_call x1, Pallas kernels, second_pivot(): pl.pallas_call(second_kernel, out_shape=TILE, in_specs=[VMEM], scratch_sh...  8.81 us
    pallas_call x1, Pallas kernels, finish(): pl.pallas_call(final_kernel, out_shape=jax.ShapeDtypeStruct(parent.shape,...  7.82 us
    ppermute x2, starting transfers between devices, on_device(): other = lambda value: lax.ppermute(value, 'core', [(0, 1), (1, 0)])  6.64 us
  transfers between devices with their start and end apart: 23, of which 11 were waited for; matrix products, arithmetic and copies ran while one was open for 9% of the time, Pallas kernels for 13%

profile of v1, /device:TPU:39, one launch (start us, length us, event | category | flops | bytes accessed | tf_op | source)
XLA Modules:
  0.0 145.0 jit_solution(1805051881081614768)
XLA Ops:
  0.0 1.0 slice.146
  1.0 1.0 fusion.12
  2.0 1.9 %collective-permute-start.1 = (bf16[512,256]{1,0:T(8,128)(2,1)S(1)}, bf16[512,256]{1,0:T(8,128)(2,1)S(1)}, u32[]{:S(2)}, u32[]{:S(2)}) collective-permute-start(bf16[512,256]{1,0:T(8,128)(2,1)S(1)} %pad_maximum_fusion.3), channel_id=1, source_target_pairs={{0,66},{64,2},{1,67},{65,3},{8,74},{72,10},{9,75},{73,11},{16,82},... | collective-permute-start | bytes 786440 | tf_op jit(solution)/shard_map/ppermute | solution.py:228
  3.9 1.4 collective-permute-start
  5.3 1.0 slice.148
  6.4 0.1 reshape.78
  6.5 0.2 compare_reduce_fusion.2
  6.7 0.2 compare_reduce_fusion
  6.9 0.1 reshape.80
  7.0 0.2 dynamic-slice_reduce_fusion.2
  7.2 0.2 compare_reduce_fusion.1
  7.5 0.1 and_convert_fusion.1
  7.6 0.1 and_convert_fusion
  7.9 0.7 slice_bitcast_fusion
  8.7 0.2 collective-permute-done.1
  8.8 1.4 collective-permute-done
  10.2 0.1 select_select_fusion.10
  10.3 7.5 %collective-permute-start.4 = (bf16[512,256]{1,0:T(8,128)(2,1)S(1)}, bf16[512,256]{1,0:T(8,128)(2,1)S(1)}, u32[]{:S(2)}, u32[]{:S(2)}) collective-permute-start(bf16[512,256]{1,0:T(8,128)(2,1)S(1)} %select_select_fusion.10), channel_id=1, source_target_pairs={{0,70},{6,4},{64,6},{70,68},{1,71},{7,5},{65,7},{71,69},{8,78},{14... | collective-permute-start | bytes 786440 | tf_op jit(solution)/shard_map/ppermute | solution.py:228
  17.8 1.9 %collective-permute-start.3 = (bf16[512,256]{1,0:T(8,128)(2,1)S(1)}, bf16[512,256]{1,0:T(8,128)(2,1)}, u32[]{:S(2)}, u32[]{:S(2)}) collective-permute-start(bf16[512,256]{1,0:T(8,128)(2,1)S(1)} %select_select_fusion.10), channel_id=1, source_target_pairs={{0,2},{6,64},{66,68},{64,66},{70,0},{2,4},{1,3},{7,65},{67,69},{65... | collective-permute-start | bytes 786440 | tf_op jit(solution)/shard_map/ppermute | solution.py:228
  19.8 0.7 fusion.13
  20.5 2.7 %collective-permute-start.2 = (bf16[256,512]{1,0:T(8,128)(2,1)S(1)}, bf16[256,512]{1,0:T(8,128)(2,1)S(1)}, u32[]{:S(2)}, u32[]{:S(2)}) collective-permute-start(bf16[256,512]{1,0:T(8,128)(2,1)S(1)} %get-tuple-element.18), channel_id=1, source_target_pairs={{0,64},{64,0},{1,65},{65,1},{2,66},{66,2},{3,67},{67,3},{4,68},{68... | collective-permute-start | bytes 786440 | tf_op jit(solution)/shard_map/ppermute | solution.py:309
  23.2 4.1 %collective-permute-done.4 = bf16[512,256]{1,0:T(8,128)(2,1)S(1)} collective-permute-done((bf16[512,256]{1,0:T(8,128)(2,1)S(1)}, bf16[512,256]{1,0:T(8,128)(2,1)S(1)}, u32[]{:S(2)}, u32[]{:S(2)}) %collective-permute-start.4) | collective-permute-done | bytes 262176 | tf_op jit(solution)/shard_map/ppermute | solution.py:228
  27.3 1.0 select_select_fusion.9
  28.3 1.3 fusion.6
  29.6 6.5 %collective-permute-start.14 = (f32[256,256]{1,0:T(8,128)S(1)}, f32[256,256]{1,0:T(8,128)}, u32[]{:S(2)}, u32[]{:S(2)}) collective-permute-start(f32[256,256]{1,0:T(8,128)S(1)} %fusion.6), channel_id=1, source_target_pairs={{0,16},{1,17},{9,25},{2,18},{3,19},{11,27},{4,20},{5,21},{13,29},{... | collective-permute-start | bytes 786440 | tf_op jit(solution)/shard_map/ppermute | solution.py:264
  36.2 4.7 %collective-permute-start.5 = (f32[256,256]{1,0:T(8,128)S(1)}, f32[256,256]{1,0:T(8,128)}, u32[]{:S(2)}, u32[]{:S(2)}) collective-permute-start(f32[256,256]{1,0:T(8,128)S(1)} %fusion.6), channel_id=1, source_target_pairs={{0,8},{1,9},{9,17},{2,10},{3,11},{11,19},{4,12},{5,13},{13,21},{6,... | collective-permute-start | bytes 786440 | tf_op jit(solution)/shard_map/ppermute | solution.py:264
  40.9 0.1 reshape.81.place
  41.1 0.2 mul.190
  41.3 0.2 mul.197
  41.6 1.4 collective-permute-start.13
  43.0 2.2 %collective-permute-start.12 = (f32[256,256]{1,0:T(8,128)S(1)}, f32[256,256]{1,0:T(8,128)S(1)}, u32[]{:S(2)}, u32[]{:S(2)}) collective-permute-start(f32[256,256]{1,0:T(8,128)S(1)} %fusion.6), channel_id=1, source_target_pairs={{0,32},{1,33},{9,41},{2,34},{3,35},{11,43},{4,36},{5,37},{13,45},{... | collective-permute-start | bytes 786440 | tf_op jit(solution)/shard_map/ppermute | solution.py:264
  45.2 1.3 collective-permute-start.11
  46.6 0.2 mul.204
  46.8 0.2 mul.211
  47.0 1.3 collective-permute-start.10
  48.4 1.9 %collective-permute-start.9 = (f32[256,256]{1,0:T(8,128)S(1)}, f32[256,256]{1,0:T(8,128)S(1)}, u32[]{:S(2)}, u32[]{:S(2)}) collective-permute-start(f32[256,256]{1,0:T(8,128)S(1)} %fusion.6), channel_id=1, source_target_pairs={{0,56},{1,57},{9,1},{2,58},{3,59},{11,3},{4,60},{5,61},{13,5},{6,6... | collective-permute-start | bytes 786440 | tf_op jit(solution)/shard_map/ppermute | solution.py:264
  50.3 0.3 fusion.3
  50.6 1.4 collective-permute-done.13
  52.0 1.9 %collective-permute-start.18 = (bf16[256,512]{1,0:T(8,128)(2,1)S(1)}, bf16[256,512]{1,0:T(8,128)(2,1)S(1)}, u32[]{:S(2)}, u32[]{:S(2)}) collective-permute-start(bf16[256,512]{1,0:T(8,128)(2,1)S(1)} %fusion.3), channel_id=1, source_target_pairs={{0,16},{8,56},{1,17},{9,57},{2,18},{10,58},{3,19},{11,59},{4,20},{... | collective-permute-start | bytes 786440 | tf_op jit(solution)/shard_map/ppermute | solution.py:228
  53.8 3.8 %collective-permute-done.12 = f32[256,256]{1,0:T(8,128)S(1)} collective-permute-done((f32[256,256]{1,0:T(8,128)S(1)}, f32[256,256]{1,0:T(8,128)S(1)}, u32[]{:S(2)}, u32[]{:S(2)}) %collective-permute-start.12) | collective-permute-done | bytes 262176 | tf_op jit(solution)/shard_map/ppermute | solution.py:264
  57.6 1.3 collective-permute-start.17
  58.9 3.8 %collective-permute-done.11 = f32[256,256]{1,0:T(8,128)S(1)} collective-permute-done((f32[256,256]{1,0:T(8,128)S(1)}, f32[256,256]{1,0:T(8,128)S(1)}, u32[]{:S(2)}, u32[]{:S(2)}) %collective-permute-start.11) | collective-permute-done | bytes 262176 | tf_op jit(solution)/shard_map/ppermute | solution.py:264
  62.7 4.7 %collective-permute-start.7 = (bf16[1024,256]{1,0:T(8,128)(2,1)S(1)}, bf16[1024,256]{1,0:T(8,128)(2,1)S(1)}, u32[]{:S(2)}, u32[]{:S(2)}) collective-permute-start(bf16[1024,256]{1,0:T(8,128)(2,1)S(1)} %pad_maximum_fusion.1), channel_id=1, source_target_pairs={{0,66},{64,2},{1,67},{65,3},{8,74},{72,10},{9,75},{73,11},{16,82},... | collective-permute-start | bytes 1572872 | tf_op jit(solution)/shard_map/ppermute | solution.py:228
  67.5 0.9 collective-permute-done.10
  68.3 3.3 %collective-permute-start.6 = (bf16[1024,256]{1,0:T(8,128)(2,1)S(1)}, bf16[1024,256]{1,0:T(8,128)(2,1)S(1)}, u32[]{:S(2)}, u32[]{:S(2)}) collective-permute-start(bf16[1024,256]{1,0:T(8,128)(2,1)S(1)} %pad_maximum_fusion.1), channel_id=1, source_target_pairs={{0,6},{64,70},{1,7},{65,71},{8,14},{72,78},{9,15},{73,79},{16,22},... | collective-permute-start | bytes 1572872 | tf_op jit(solution)/shard_map/ppermute | solution.py:228
  71.6 5.1 %collective-permute-done.9 = f32[256,256]{1,0:T(8,128)S(1)} collective-permute-done((f32[256,256]{1,0:T(8,128)S(1)}, f32[256,256]{1,0:T(8,128)S(1)}, u32[]{:S(2)}, u32[]{:S(2)}) %collective-permute-start.9) | collective-permute-done | bytes 262176 | tf_op jit(solution)/shard_map/ppermute | solution.py:264
  76.8 1.2 select_select_fusion.7
  78.0 2.6 %collective-permute-start.19 = (f32[512,256]{1,0:T(8,128)S(1)}, f32[512,256]{1,0:T(8,128)S(1)}, u32[]{:S(2)}, u32[]{:S(2)}) collective-permute-start(f32[512,256]{1,0:T(8,128)S(1)} %pad_maximum_fusion.2.mine_ref), channel_id=1, source_target_pairs={{0,1},{1,0},{2,3},{3,2},{4,5},{5,4},{6,7},{7,6},{8,9},{9,8},{10,11... | collective-permute-start | bytes 1572872 | tf_op jit(solution)/shard_map/ppermute | solution.py:283
  80.7 1.7 %collective-permute-done.17 = bf16[256,512]{1,0:T(8,128)(2,1)S(1)} collective-permute-done((bf16[256,512]{1,0:T(8,128)(2,1)S(1)}, bf16[256,512]{1,0:T(8,128)(2,1)S(1)}, u32[]{:S(2)}, u32[]{:S(2)}) %collective-permute-start.17) | collective-permute-done | bytes 262176 | tf_op jit(solution)/shard_map/ppermute | solution.py:228
  82.4 3.6 %collective-permute-start.22 = (bf16[256,512]{1,0:T(8,128)(2,1)S(1)}, bf16[256,512]{1,0:T(8,128)(2,1)S(1)}, u32[]{:S(2)}, u32[]{:S(2)}) collective-permute-start(bf16[256,512]{1,0:T(8,128)(2,1)S(1)} %select_select_fusion.5), channel_id=1, source_target_pairs={{0,56},{40,48},{8,0},{32,24},{1,57},{41,49},{9,1},{33,25},{2,58},{... | collective-permute-start | bytes 786440 | tf_op jit(solution)/shard_map/ppermute | solution.py:228
  86.1 2.2 %collective-permute-start.21 = (bf16[256,512]{1,0:T(8,128)(2,1)S(1)}, bf16[256,512]{1,0:T(8,128)(2,1)S(1)}, u32[]{:S(2)}, u32[]{:S(2)}) collective-permute-start(bf16[256,512]{1,0:T(8,128)(2,1)S(1)} %select_select_fusion.5), channel_id=1, source_target_pairs={{0,8},{40,32},{16,24},{8,16},{32,40},{56,48},{1,9},{41,33},{17,25}... | collective-permute-start | bytes 786440 | tf_op jit(solution)/shard_map/ppermute | solution.py:228
  88.3 0.1 select_select_fusion.2
  88.4 5.0 %collective-permute-start.16 = (bf16[1024,256]{1,0:T(8,128)(2,1)S(1)}, bf16[1024,256]{1,0:T(8,128)(2,1)S(1)}, u32[]{:S(2)}, u32[]{:S(2)}) collective-permute-start(bf16[1024,256]{1,0:T(8,128)(2,1)S(1)} %select_select_fusion.2), channel_id=1, source_target_pairs={{0,70},{6,4},{64,6},{70,68},{1,71},{7,5},{65,7},{71,69},{8,78},{14... | collective-permute-start | bytes 1572872 | tf_op jit(solution)/shard_map/ppermute | solution.py:228
  93.4 1.9 %collective-permute-start.15 = (bf16[1024,256]{1,0:T(8,128)(2,1)S(1)}, bf16[1024,256]{1,0:T(8,128)(2,1)S(1)}, u32[]{:S(2)}, u32[]{:S(2)}) collective-permute-start(bf16[1024,256]{1,0:T(8,128)(2,1)S(1)} %select_select_fusion.2), channel_id=1, source_target_pairs={{0,2},{6,64},{66,68},{64,66},{70,0},{2,4},{1,3},{7,65},{67,69},{65... | collective-permute-start | bytes 1572872 | tf_op jit(solution)/shard_map/ppermute | solution.py:228
  95.3 2.3 %collective-permute-start.8 = (bf16[256,512]{1,0:T(8,128)(2,1)S(1)}, bf16[256,512]{1,0:T(8,128)(2,1)S(1)}, u32[]{:S(2)}, u32[]{:S(2)}) collective-permute-start(bf16[256,512]{1,0:T(8,128)(2,1)S(1)} %copy-done.3), channel_id=1, source_target_pairs={{0,64},{64,0},{1,65},{65,1},{2,66},{66,2},{3,67},{67,3},{4,68},{68... | collective-permute-start | bytes 786440 | tf_op jit(solution)/shard_map/ppermute | solution.py:309
  97.6 10.5 %shard_map.46 = (f32[256,256]{1,0:T(8,128)S(1)}, f32[256,256]{1,0:T(8,128)S(1)}, f32[256,256]{1,0:T(8,128)S(1)}) custom-call(s32[3]{0:T(128)S(1)} %pad_add_fusion.where, f32[512,256]{1,0:T(8,128)S(1)} %pad_maximum_fusion.2.mine_ref, f32[512,256]{1,0:T(8,128)S(1)} %collective-permute-done.19.theirs_ref), custom_call_target="tpu_custom_call" | custom-call | flops 10000000000 | bytes 1048576 | tf_op jit(solution)/shard_map/pallas_call | solution.py:113
  108.1 1.0 collective-permute-done.16
  109.1 11.1 %collective-permute-done.15 = bf16[1024,256]{1,0:T(8,128)(2,1)S(1)} collective-permute-done((bf16[1024,256]{1,0:T(8,128)(2,1)S(1)}, bf16[1024,256]{1,0:T(8,128)(2,1)S(1)}, u32[]{:S(2)}, u32[]{:S(2)}) %collective-permute-start.15) | collective-permute-done | bytes 524320 | tf_op jit(solution)/shard_map/ppermute | solution.py:228
  120.2 0.1 select_select_fusion.1
  120.3 0.1 fusion.4
  120.4 3.8 %fusion.8 = (f32[256,256]{1,0:T(8,128)S(1)}, f32[256,256]{1,0:T(8,128)S(1)}, f32[256,256]{1,0:T(8,128)S(1)}) fusion(f32[768,256]{1,0:T(8,128)S(1)} %fusion.4, f32[]{:T(128)} %bitcast.11, f32[]{:T(128)} %bitcast.10, bf16[512,256]{1,0:T(8,128)(2,1)S(1)} %get-tuple-element.45, bf16[512,256]{1,0:T(8,128)(2,1)S(1)} %get-tuple-element.44, f32[]{:T(128)} %bitcast.13, ...), kind=kLoop, calls=%fused_computation.22 | loop fusion | flops 1048576 | bytes 2097176 | tf_op jit(solution)/shard_map/add | solution.py:336
  124.3 4.0 %collective-permute-start.20 = (f32[1024,256]{1,0:T(8,128)S(1)}, f32[1024,256]{1,0:T(8,128)S(1)}, u32[]{:S(2)}, u32[]{:S(2)}) collective-permute-start(f32[1024,256]{1,0:T(8,128)S(1)} %pad_maximum_fusion.mine_ref), channel_id=1, source_target_pairs={{0,1},{1,0},{2,3},{3,2},{4,5},{5,4},{6,7},{7,6},{8,9},{9,8},{10,11... | collective-permute-start | bytes 3145736 | tf_op jit(solution)/shard_map/ppermute | solution.py:283
  128.4 8.8 %shard_map.47.x1_ref = f32[256,256]{1,0:T(8,128)S(1)} custom-call(f32[256,256]{1,0:T(8,128)S(1)} %get-tuple-element.29.rest_ref), custom_call_target="tpu_custom_call" | custom-call | flops 10000000000 | bytes 1048576 | tf_op jit(solution)/shard_map/pallas_call | solution.py:124
  137.2 7.8 %shard_map.48 = f32[1024,512]{1,0:T(8,128)} custom-call(f32[64]{0:T(128)S(1)} %reshape.81.place, s32[3]{0:T(128)S(1)} %pad_add_fusion.where, bf16[1024,512]{1,0:T(8,128)(2,1)S(1)} %bitcast.55, bf16[512,512]{1,0:T(8,128)(2,1)S(1)} %bitcast.52, bf16[256,512]{1,0:T(8,128)(2,1)S(1)} %collective-permute-done.2.top_ref, ...), custom_call_target="tpu_custom_call" | custom-call | tf_op jit(solution)/shard_map/pallas_call | solution.py:193
  (49 shorter events, 0.9 us)
Async XLA Ops:
  0.0 6.5 %copy-start = (s32[8,16,16]{2,1,0:T(8,128)S(1)}, s32[8,16,16]{2,1,0:T(8,128)}, u32[]{:S(2)}) copy-start(s32[8,16,16]{2,1,0:T(8,128)} %param.7) | copy-start | bytes 24580
  0.0 7.9 %copy-start.1 = (bf16[1,512,512]{2,1,0:T(8,128)(2,1)S(1)}, bf16[1,512,512]{2,1,0:T(8,128)(2,1)}, u32[]{:S(2)}) copy-start(bf16[1,512,512]{2,1,0:T(8,128)(2,1)} %param.5) | copy-start | bytes 1572868
  0.0 6.3 %copy-start.4 = (s32[8,16]{1,0:T(8,128)S(1)}, s32[8,16]{1,0:T(8,128)}, u32[]{:S(2)}) copy-start(s32[8,16]{1,0:T(8,128)} %param.6) | copy-start | bytes 1540
  2.0 6.8 %collective-permute-start.1 = (bf16[512,256]{1,0:T(8,128)(2,1)S(1)}, bf16[512,256]{1,0:T(8,128)(2,1)S(1)}, u32[]{:S(2)}, u32[]{:S(2)}) collective-permute-start(bf16[512,256]{1,0:T(8,128)(2,1)S(1)} %pad_maximum_fusion.3), channel_id=1, source_target_pairs={{0,66},{64,2},{1,67},{65,3},{8,74},{72,10},{9,75},{73,11},{16,82},... | collective-permute-start | bytes 786440 | tf_op jit(solution)/shard_map/ppermute | solution.py:228
  3.9 6.3 %collective-permute-start = (bf16[512,256]{1,0:T(8,128)(2,1)S(1)}, bf16[512,256]{1,0:T(8,128)(2,1)S(1)}, u32[]{:S(2)}, u32[]{:S(2)}) collective-permute-start(bf16[512,256]{1,0:T(8,128)(2,1)S(1)} %pad_maximum_fusion.3), channel_id=1, source_target_pairs={{0,6},{64,70},{1,7},{65,71},{8,14},{72,78},{9,15},{73,79},{16,22},... | collective-permute-start | bytes 786440 | tf_op jit(solution)/shard_map/ppermute | solution.py:228
  10.3 17.0 %collective-permute-start.4 = (bf16[512,256]{1,0:T(8,128)(2,1)S(1)}, bf16[512,256]{1,0:T(8,128)(2,1)S(1)}, u32[]{:S(2)}, u32[]{:S(2)}) collective-permute-start(bf16[512,256]{1,0:T(8,128)(2,1)S(1)} %select_select_fusion.10), channel_id=1, source_target_pairs={{0,70},{6,4},{64,6},{70,68},{1,71},{7,5},{65,7},{71,69},{8,78},{14... | collective-permute-start | bytes 786440 | tf_op jit(solution)/shard_map/ppermute | solution.py:228
  17.8 9.5 %collective-permute-start.3 = (bf16[512,256]{1,0:T(8,128)(2,1)S(1)}, bf16[512,256]{1,0:T(8,128)(2,1)}, u32[]{:S(2)}, u32[]{:S(2)}) collective-permute-start(bf16[512,256]{1,0:T(8,128)(2,1)S(1)} %select_select_fusion.10), channel_id=1, source_target_pairs={{0,2},{6,64},{66,68},{64,66},{70,0},{2,4},{1,3},{7,65},{67,69},{65... | collective-permute-start | bytes 786440 | tf_op jit(solution)/shard_map/ppermute | solution.py:228
  20.5 24.7 %collective-permute-start.2 = (bf16[256,512]{1,0:T(8,128)(2,1)S(1)}, bf16[256,512]{1,0:T(8,128)(2,1)S(1)}, u32[]{:S(2)}, u32[]{:S(2)}) collective-permute-start(bf16[256,512]{1,0:T(8,128)(2,1)S(1)} %get-tuple-element.18), channel_id=1, source_target_pairs={{0,64},{64,0},{1,65},{65,1},{2,66},{66,2},{3,67},{67,3},{4,68},{68... | collective-permute-start | bytes 786440 | tf_op jit(solution)/shard_map/ppermute | solution.py:309
  29.6 17.4 %collective-permute-start.14 = (f32[256,256]{1,0:T(8,128)S(1)}, f32[256,256]{1,0:T(8,128)}, u32[]{:S(2)}, u32[]{:S(2)}) collective-permute-start(f32[256,256]{1,0:T(8,128)S(1)} %fusion.6), channel_id=1, source_target_pairs={{0,16},{1,17},{9,25},{2,18},{3,19},{11,27},{4,20},{5,21},{13,29},{... | collective-permute-start | bytes 786440 | tf_op jit(solution)/shard_map/ppermute | solution.py:264
  36.2 12.2 %collective-permute-start.5 = (f32[256,256]{1,0:T(8,128)S(1)}, f32[256,256]{1,0:T(8,128)}, u32[]{:S(2)}, u32[]{:S(2)}) collective-permute-start(f32[256,256]{1,0:T(8,128)S(1)} %fusion.6), channel_id=1, source_target_pairs={{0,8},{1,9},{9,17},{2,10},{3,11},{11,19},{4,12},{5,13},{13,21},{6,... | collective-permute-start | bytes 786440 | tf_op jit(solution)/shard_map/ppermute | solution.py:264
  41.6 8.7 %copy-start.2 = (bf16[1,1024,512]{2,1,0:T(8,128)(2,1)S(1)}, bf16[1,1024,512]{2,1,0:T(8,128)(2,1)}, u32[]{:S(2)}) copy-start(bf16[1,1024,512]{2,1,0:T(8,128)(2,1)} %param.4) | copy-start | bytes 3145732
  41.6 10.4 %collective-permute-start.13 = (f32[256,256]{1,0:T(8,128)S(1)}, f32[256,256]{1,0:T(8,128)S(1)}, u32[]{:S(2)}, u32[]{:S(2)}) collective-permute-start(f32[256,256]{1,0:T(8,128)S(1)} %fusion.6), channel_id=1, source_target_pairs={{0,24},{1,25},{9,33},{2,26},{3,27},{11,35},{4,28},{5,29},{13,37},{... | collective-permute-start | bytes 786440 | tf_op jit(solution)/shard_map/ppermute | solution.py:264
  43.0 14.6 %collective-permute-start.12 = (f32[256,256]{1,0:T(8,128)S(1)}, f32[256,256]{1,0:T(8,128)S(1)}, u32[]{:S(2)}, u32[]{:S(2)}) collective-permute-start(f32[256,256]{1,0:T(8,128)S(1)} %fusion.6), channel_id=1, source_target_pairs={{0,32},{1,33},{9,41},{2,34},{3,35},{11,43},{4,36},{5,37},{13,45},{... | collective-permute-start | bytes 786440 | tf_op jit(solution)/shard_map/ppermute | solution.py:264
  45.2 17.5 %collective-permute-start.11 = (f32[256,256]{1,0:T(8,128)S(1)}, f32[256,256]{1,0:T(8,128)S(1)}, u32[]{:S(2)}, u32[]{:S(2)}) collective-permute-start(f32[256,256]{1,0:T(8,128)S(1)} %fusion.6), channel_id=1, source_target_pairs={{0,40},{1,41},{9,49},{2,42},{3,43},{11,51},{4,44},{5,45},{13,53},{... | collective-permute-start | bytes 786440 | tf_op jit(solution)/shard_map/ppermute | solution.py:264
  47.0 21.3 %collective-permute-start.10 = (f32[256,256]{1,0:T(8,128)S(1)}, f32[256,256]{1,0:T(8,128)S(1)}, u32[]{:S(2)}, u32[]{:S(2)}) collective-permute-start(f32[256,256]{1,0:T(8,128)S(1)} %fusion.6), channel_id=1, source_target_pairs={{0,48},{1,49},{9,57},{2,50},{3,51},{11,59},{4,52},{5,53},{13,61},{... | collective-permute-start | bytes 786440 | tf_op jit(solution)/shard_map/ppermute | solution.py:264
  48.4 28.4 %collective-permute-start.9 = (f32[256,256]{1,0:T(8,128)S(1)}, f32[256,256]{1,0:T(8,128)S(1)}, u32[]{:S(2)}, u32[]{:S(2)}) collective-permute-start(f32[256,256]{1,0:T(8,128)S(1)} %fusion.6), channel_id=1, source_target_pairs={{0,56},{1,57},{9,1},{2,58},{3,59},{11,3},{4,60},{5,61},{13,5},{6,6... | collective-permute-start | bytes 786440 | tf_op jit(solution)/shard_map/ppermute | solution.py:264
  52.0 28.7 %collective-permute-start.18 = (bf16[256,512]{1,0:T(8,128)(2,1)S(1)}, bf16[256,512]{1,0:T(8,128)(2,1)S(1)}, u32[]{:S(2)}, u32[]{:S(2)}) collective-permute-start(bf16[256,512]{1,0:T(8,128)(2,1)S(1)} %fusion.3), channel_id=1, source_target_pairs={{0,16},{8,56},{1,17},{9,57},{2,18},{10,58},{3,19},{11,59},{4,20},{... | collective-permute-start | bytes 786440 | tf_op jit(solution)/shard_map/ppermute | solution.py:228
  57.6 24.8 %collective-permute-start.17 = (bf16[256,512]{1,0:T(8,128)(2,1)S(1)}, bf16[256,512]{1,0:T(8,128)(2,1)S(1)}, u32[]{:S(2)}, u32[]{:S(2)}) collective-permute-start(bf16[256,512]{1,0:T(8,128)(2,1)S(1)} %fusion.3), channel_id=1, source_target_pairs={{0,40},{8,32},{1,41},{9,33},{2,42},{10,34},{3,43},{11,35},{4,44},{... | collective-permute-start | bytes 786440 | tf_op jit(solution)/shard_map/ppermute | solution.py:228
  62.7 25.5 %collective-permute-start.7 = (bf16[1024,256]{1,0:T(8,128)(2,1)S(1)}, bf16[1024,256]{1,0:T(8,128)(2,1)S(1)}, u32[]{:S(2)}, u32[]{:S(2)}) collective-permute-start(bf16[1024,256]{1,0:T(8,128)(2,1)S(1)} %pad_maximum_fusion.1), channel_id=1, source_target_pairs={{0,66},{64,2},{1,67},{65,3},{8,74},{72,10},{9,75},{73,11},{16,82},... | collective-permute-start | bytes 1572872 | tf_op jit(solution)/shard_map/ppermute | solution.py:228
  68.3 19.9 %collective-permute-start.6 = (bf16[1024,256]{1,0:T(8,128)(2,1)S(1)}, bf16[1024,256]{1,0:T(8,128)(2,1)S(1)}, u32[]{:S(2)}, u32[]{:S(2)}) collective-permute-start(bf16[1024,256]{1,0:T(8,128)(2,1)S(1)} %pad_maximum_fusion.1), channel_id=1, source_target_pairs={{0,6},{64,70},{1,7},{65,71},{8,14},{72,78},{9,15},{73,79},{16,22},... | collective-permute-start | bytes 1572872 | tf_op jit(solution)/shard_map/ppermute | solution.py:228
  78.0 17.4 %copy-start.3 = (bf16[256,512]{1,0:T(8,128)(2,1)S(1)}, bf16[256,512]{1,0:T(8,128)(2,1)}, u32[]{:S(2)}) copy-start(bf16[256,512]{1,0:T(8,128)(2,1)} %get-tuple-element.20) | copy-start | bytes 786436
  78.0 17.3 %collective-permute-start.19 = (f32[512,256]{1,0:T(8,128)S(1)}, f32[512,256]{1,0:T(8,128)S(1)}, u32[]{:S(2)}, u32[]{:S(2)}) collective-permute-start(f32[512,256]{1,0:T(8,128)S(1)} %pad_maximum_fusion.2.mine_ref), channel_id=1, source_target_pairs={{0,1},{1,0},{2,3},{3,2},{4,5},{5,4},{6,7},{7,6},{8,9},{9,8},{10,11... | collective-permute-start | bytes 1572872 | tf_op jit(solution)/shard_map/ppermute | solution.py:283
  82.4 45.9 %collective-permute-start.22 = (bf16[256,512]{1,0:T(8,128)(2,1)S(1)}, bf16[256,512]{1,0:T(8,128)(2,1)S(1)}, u32[]{:S(2)}, u32[]{:S(2)}) collective-permute-start(bf16[256,512]{1,0:T(8,128)(2,1)S(1)} %select_select_fusion.5), channel_id=1, source_target_pairs={{0,56},{40,48},{8,0},{32,24},{1,57},{41,49},{9,1},{33,25},{2,58},{... | collective-permute-start | bytes 786440 | tf_op jit(solution)/shard_map/ppermute | solution.py:228
  86.1 42.3 %collective-permute-start.21 = (bf16[256,512]{1,0:T(8,128)(2,1)S(1)}, bf16[256,512]{1,0:T(8,128)(2,1)S(1)}, u32[]{:S(2)}, u32[]{:S(2)}) collective-permute-start(bf16[256,512]{1,0:T(8,128)(2,1)S(1)} %select_select_fusion.5), channel_id=1, source_target_pairs={{0,8},{40,32},{16,24},{8,16},{32,40},{56,48},{1,9},{41,33},{17,25}... | collective-permute-start | bytes 786440 | tf_op jit(solution)/shard_map/ppermute | solution.py:228
  88.4 20.7 %collective-permute-start.16 = (bf16[1024,256]{1,0:T(8,128)(2,1)S(1)}, bf16[1024,256]{1,0:T(8,128)(2,1)S(1)}, u32[]{:S(2)}, u32[]{:S(2)}) collective-permute-start(bf16[1024,256]{1,0:T(8,128)(2,1)S(1)} %select_select_fusion.2), channel_id=1, source_target_pairs={{0,70},{6,4},{64,6},{70,68},{1,71},{7,5},{65,7},{71,69},{8,78},{14... | collective-permute-start | bytes 1572872 | tf_op jit(solution)/shard_map/ppermute | solution.py:228
  93.4 26.8 %collective-permute-start.15 = (bf16[1024,256]{1,0:T(8,128)(2,1)S(1)}, bf16[1024,256]{1,0:T(8,128)(2,1)S(1)}, u32[]{:S(2)}, u32[]{:S(2)}) collective-permute-start(bf16[1024,256]{1,0:T(8,128)(2,1)S(1)} %select_select_fusion.2), channel_id=1, source_target_pairs={{0,2},{6,64},{66,68},{64,66},{70,0},{2,4},{1,3},{7,65},{67,69},{65... | collective-permute-start | bytes 1572872 | tf_op jit(solution)/shard_map/ppermute | solution.py:228
  95.3 41.9 %collective-permute-start.8 = (bf16[256,512]{1,0:T(8,128)(2,1)S(1)}, bf16[256,512]{1,0:T(8,128)(2,1)S(1)}, u32[]{:S(2)}, u32[]{:S(2)}) collective-permute-start(bf16[256,512]{1,0:T(8,128)(2,1)S(1)} %copy-done.3), channel_id=1, source_target_pairs={{0,64},{64,0},{1,65},{65,1},{2,66},{66,2},{3,67},{67,3},{4,68},{68... | collective-permute-start | bytes 786440 | tf_op jit(solution)/shard_map/ppermute | solution.py:309
  124.3 12.9 %collective-permute-start.20 = (f32[1024,256]{1,0:T(8,128)S(1)}, f32[1024,256]{1,0:T(8,128)S(1)}, u32[]{:S(2)}, u32[]{:S(2)}) collective-permute-start(f32[1024,256]{1,0:T(8,128)S(1)} %pad_maximum_fusion.mine_ref), channel_id=1, source_target_pairs={{0,1},{1,0},{2,3},{3,2},{4,5},{5,4},{6,7},{7,6},{8,9},{9,8},{10,11... | collective-permute-start | bytes 3145736 | tf_op jit(solution)/shard_map/ppermute | solution.py:283

commit v2 on v1

--- a/solution.py
+++ b/solution.py
@@ -132,7 +132,7 @@
 
 
 def final_kernel(
-    place, where, parent_ref, own_ref, top_ref, low_ref, mine_ref, theirs_ref, g_ref, h_ref,
+    place, where, parent_ref, own_ref, sib_ref, mine_ref, theirs_ref, g_ref, h_ref,
     x0_ref, x1_ref, l10_ref, out_ref, across, xs,
 ):
     slot = pl.program_id(0)
@@ -165,9 +165,8 @@
         value = parent_ref[:, cols].astype(F32)
         for b in range(v + 1):
             here = slice(b * B, (b + 1) * B)
-            sib = jnp.where(last == 1, low_ref[:, here].astype(F32), top_ref[:, here].astype(F32))
-            own = own_ref[pl.ds(from_row, B), here].astype(F32)
-            for child, part in enumerate((own, sib)):
+            for child, ref in enumerate((own_ref, sib_ref)):
+                part = ref[pl.ds(from_row, B), here].astype(F32)
                 w = place[(((child * 2 + last) * 2 + b) * 4 + slot) * 2 + v]
                 value += w * part
         q0, q1 = across[0:B, cols], across[B:, cols]
@@ -186,7 +185,7 @@
         out_ref[:, 0:B] = jnp.where(keep, p1, 0.0)
 
 
-def finish(place, where, parent, own, top, low, mine, theirs, g, h, x0, x1, l10):
+def finish(place, where, parent, own, sib, mine, theirs, g, h, x0, x1, l10):
     whole = lambda shape: pl.BlockSpec(shape, lambda i, *_: (0, 0))
     rows = lambda width: pl.BlockSpec((B, width), lambda i, *_: (i, 0))
     wide, tile = whole((B, 2 * B)), whole((B, B))
@@ -197,14 +196,14 @@
             num_scalar_prefetch=2,
             grid=(parent.shape[0] // B,),
             in_specs=[
-                rows(2 * B), whole((2 * B, 2 * B)), wide, wide, rows(B), rows(B),
+                rows(2 * B), whole((2 * B, 2 * B)), whole((2 * B, 2 * B)), rows(B), rows(B),
                 wide, wide, tile, tile, tile,
             ],
             out_specs=rows(2 * B),
             scratch_shapes=[pltpu.VMEM((2 * B, 2 * B), BF16), pltpu.VMEM((6, B, B), BF16)],
         ),
         compiler_params=pltpu.CompilerParams(vmem_limit_bytes=48 * 2**20),
-    )(place, where, parent, own, top, low, mine, theirs, g, h, x0, x1, l10)
+    )(place, where, parent, own, sib, mine, theirs, g, h, x0, x1, l10)
 
 
 def tie(value, *after):
@@ -256,21 +255,6 @@
         [(0, 1), (5, 4), (2, 3), (1, 2), (4, 5), (7, 6)], [(0, 7), (5, 6), (1, 0), (4, 3)],
         ((0, 2, 5), (1, 3, 4)), ((1, 4, 7), (2, 5, 6)),
     )
-
-
-def direct_z(block, z, before_last):
-    late = tie(block, before_last)
-    recv = [
-        lax.ppermute(
-            block if s < 5 else late, ("row", "core"), [(0, 2 * s), (1, 2 * s + 1), (3, 2 * ((1 + s) % 8) + 1)]
-        )
-        for s in range(1, 8)
-    ]
-    zero, one = block, block
-    for s in range(1, 8):
-        zero = jnp.where(z == s, recv[s - 1], zero)
-        one = jnp.where(z == (1 + s) % 8, recv[s - 1], one)
-    return jnp.concatenate([zero, one], axis=0), recv[0]
 
 
 def on_device(parent, child, child_blocks, child_mask):
@@ -314,23 +298,22 @@
     base = jnp.where(core == 0, from0[:B], from4[:B]).astype(F32)
     childs = [from0[B:].astype(F32), from4[B:].astype(F32)]
     top = base + panel_place[0, 0, 0] * childs[0] + panel_place[1, 0, 0] * childs[1]
-    sib_top = swap(tie(child[:B], held))
-    pivot_rows, early = direct_z(top, z, sib_top)
-    theirs = other(pivot_rows)
-
+    sibling = swap(tie(child, held))
     rest = jnp.concatenate([parent[B:, :B], child[B:, :B]], axis=0)
-    rest_held = spread_y.start(tie(rest, early))
+    rest_held = spread_y.start(tie(rest, held))
+    top_held = spread_z.start(top)
+    pivot_rows = jnp.concatenate(spread_z.end(tie(top_held, rest_held)), axis=0)
+    theirs = other(tie(pivot_rows, sibling))
 
     strip = parent[:B].astype(F32).reshape(B, 2, B)
-    for k, ref in ((0, child[:B]), (1, sib_top)):
+    for k, ref in ((0, child[:B]), (1, sibling[:B])):
         for b in range(2):
             strip += place[k, 0, b, 0][None, :, None] * ref[:, None, b * B : (b + 1) * B].astype(F32)
-    strip_held = spread_z.start(tie(strip.reshape(B, 2 * B).astype(BF16), early))
+    strip_held = spread_z.start(tie(strip.reshape(B, 2 * B).astype(BF16), pivot_rows))
     rest0, rest4 = spread_y.end(tie(rest_held, pivot_rows))
 
-    x0, l10, low = first_pivot(tie(where, strip_held), pivot_rows, theirs)
-    g, h = spread_z.end(tie(strip_held, pivot_rows))
-    sib_low = swap(tie(child[B:], rest_held))
+    x0, l10, low = first_pivot(where, pivot_rows, theirs)
+    g, h = spread_z.end(tie(strip_held, x0))
     tiles = jnp.where(core == 0, rest0[: 3 * B], rest4[: 3 * B]).astype(F32)
     below = [
         tiles[(s - 1) * B : s * B]
@@ -342,7 +325,7 @@
     column_other = other(tie(column, x0))
     x1 = second_pivot(tie(low, column))
     out = finish(
-        place.reshape(-1), where, parent, child, sib_top, sib_low, column, column_other,
+        place.reshape(-1), where, parent, child, sibling, column, column_other,
         g, h, x0, x1, l10,
     )
     return out[None]

time: 146 us -> 137 us (0.938)
  the two profiles are of different devices: /device:TPU:39 before, /device:TPU:11 now
where the time goes in v2:
time: 137 us
  starting transfers between devices  66.7 us (49%)
  Pallas kernels  26.8 us (20%)
  waiting for transfers between devices  25.7 us (19%)
  other arithmetic  9.78 us (7%)
  local copies, waits for them, and re-layouts  6.95 us (5%)
    ppermute x16, starting transfers between devices, send(): return lax.ppermute(value, self.axes, self.routes[k])  49.9 us
    ppermute x16, waiting for transfers between devices, send(): return lax.ppermute(value, self.axes, self.routes[k])  25.7 us
    pallas_call x1, Pallas kernels, first_pivot(): pl.pallas_call(first_kernel, out_shape=(TILE, TILE, TILE), in_specs=[pl.B...  10.5 us
    ppermute x2, starting transfers between devices, on_device(): other = lambda value: lax.ppermute(value, 'core', [(0, 1), (1, 0)])  10.2 us
    pallas_call x1, Pallas kernels, second_pivot(): pl.pallas_call(second_kernel, out_shape=TILE, in_specs=[VMEM], scratch_sh...  8.81 us
    pallas_call x1, Pallas kernels, finish(): pl.pallas_call(final_kernel, out_shape=jax.ShapeDtypeStruct(parent.shape,...  7.57 us
    ppermute x1, starting transfers between devices, on_device(): swap = lambda value: lax.ppermute(value, 'y_hi', [(0, 1), (1, 0)])  6.5 us
    add x1, other arithmetic, on_device(): tiles[(s - 1) * B:s * B]  3.82 us
  transfers between devices with their start and end apart: 19, of which 6 were waited for; matrix products, arithmetic and copies ran while one was open for 11% of the time, Pallas kernels for 14%

profile of v2, /device:TPU:11, one launch (start us, length us, event | category | flops | bytes accessed | tf_op | source)
XLA Modules:
  0.0 136.6 jit_solution(2129901165370605787)
XLA Ops:
  0.0 1.0 slice.140
  1.0 0.0 copy-start.2
  1.0 1.0 fusion.12
  2.1 1.3 collective-permute-start.1
  3.4 0.7 collective-permute-start
  4.1 1.0 slice.148
  5.2 0.1 reshape.77
  5.3 0.2 compare_reduce_fusion.2
  5.5 0.2 compare_reduce_fusion
  5.7 0.1 reshape.79
  5.8 0.2 dynamic-slice_reduce_fusion.2
  6.0 0.2 compare_reduce_fusion.1
  6.2 0.1 broadcast_compare_fusion
  6.3 0.1 and_convert_fusion.1
  6.4 0.1 and_convert_fusion
  6.6 7.6 %collective-permute-done.1 = bf16[512,256]{1,0:T(8,128)(2,1)S(1)} collective-permute-done((bf16[512,256]{1,0:T(8,128)(2,1)S(1)}, bf16[512,256]{1,0:T(8,128)(2,1)S(1)}, u32[]{:S(2)}, u32[]{:S(2)}) %collective-permute-start.1) | collective-permute-done | bytes 262176 | tf_op jit(solution)/shard_map/ppermute | solution.py:227
  14.1 0.1 select_select_fusion.11
  14.2 0.7 collective-permute-start.4
  14.9 1.9 %collective-permute-start.3 = (bf16[512,256]{1,0:T(8,128)(2,1)S(1)}, bf16[512,256]{1,0:T(8,128)(2,1)S(1)}, u32[]{:S(2)}, u32[]{:S(2)}) collective-permute-start(bf16[512,256]{1,0:T(8,128)(2,1)S(1)} %select_select_fusion.11), channel_id=1, source_target_pairs={{0,2},{6,64},{66,68},{64,66},{70,0},{2,4},{1,3},{7,65},{67,69},{65... | collective-permute-start | bytes 786440 | tf_op jit(solution)/shard_map/ppermute | solution.py:227
  16.8 0.7 fusion.13
  17.6 1.3 collective-permute-start.6
  18.9 1.5 %collective-permute-start.5 = (bf16[1024,256]{1,0:T(8,128)(2,1)S(1)}, bf16[1024,256]{1,0:T(8,128)(2,1)}, u32[]{:S(2)}, u32[]{:S(2)}) collective-permute-start(bf16[1024,256]{1,0:T(8,128)(2,1)S(1)} %pad_maximum_fusion.1), channel_id=1, source_target_pairs={{0,6},{64,70},{1,7},{65,71},{8,14},{72,78},{9,15},{73,79},{16,22},... | collective-permute-start | bytes 1572872 | tf_op jit(solution)/shard_map/ppermute | solution.py:227
  20.3 5.3 %collective-permute-done.3 = bf16[512,256]{1,0:T(8,128)(2,1)S(1)} collective-permute-done((bf16[512,256]{1,0:T(8,128)(2,1)S(1)}, bf16[512,256]{1,0:T(8,128)(2,1)S(1)}, u32[]{:S(2)}, u32[]{:S(2)}) %collective-permute-start.3) | collective-permute-done | bytes 262176 | tf_op jit(solution)/shard_map/ppermute | solution.py:227
  25.8 1.4 %fusion.6 = f32[256,256]{1,0:T(8,128)S(1)} fusion(bf16[512,256]{1,0:T(8,128)(2,1)S(1)} %get-tuple-element.43, bf16[512,256]{1,0:T(8,128)(2,1)S(1)} %get-tuple-element.42, f32[]{:T(128)} %bitcast.7, f32[]{:T(128)} %bitcast.6, pred[]{:T(512)S(6)} %eq.182), kind=kLoop, calls=%fused_computation.20 | loop fusion | flops 524288 | bytes 786441 | tf_op jit(solution)/shard_map/add | solution.py:300
  27.2 5.8 %collective-permute-start.8 = (f32[256,256]{1,0:T(8,128)S(1)}, f32[256,256]{1,0:T(8,128)S(1)}, u32[]{:S(2)}, u32[]{:S(2)}) collective-permute-start(f32[256,256]{1,0:T(8,128)S(1)} %fusion.6), channel_id=1, source_target_pairs={{0,16},{8,56},{1,17},{9,57},{2,18},{10,58},{3,19},{11,59},{4,20},{... | collective-permute-start | bytes 786440 | tf_op jit(solution)/shard_map/ppermute | solution.py:227
  33.0 6.2 %collective-permute-start.7 = (f32[256,256]{1,0:T(8,128)S(1)}, f32[256,256]{1,0:T(8,128)}, u32[]{:S(2)}, u32[]{:S(2)}) collective-permute-start(f32[256,256]{1,0:T(8,128)S(1)} %fusion.6), channel_id=1, source_target_pairs={{0,40},{8,32},{1,41},{9,33},{2,42},{10,34},{3,43},{11,35},{4,44},{... | collective-permute-start | bytes 786440 | tf_op jit(solution)/shard_map/ppermute | solution.py:227
  39.2 0.1 broadcast_bitcast_fusion.2
  39.4 6.5 %collective-permute-start.2 = (bf16[512,512]{1,0:T(8,128)(2,1)S(1)}, bf16[512,512]{1,0:T(8,128)(2,1)S(1)}, u32[]{:S(2)}, u32[]{:S(2)}) collective-permute-start(bf16[512,512]{1,0:T(8,128)(2,1)S(1)} %bitcast.53), channel_id=1, source_target_pairs={{0,64},{64,0},{1,65},{65,1},{2,66},{66,2},{3,67},{67,3},{4,68},{68... | collective-permute-start | bytes 1572872 | tf_op jit(solution)/shard_map/ppermute | solution.py:293
  45.9 4.1 %collective-permute-done.7 = f32[256,256]{1,0:T(8,128)} collective-permute-done((f32[256,256]{1,0:T(8,128)S(1)}, f32[256,256]{1,0:T(8,128)}, u32[]{:S(2)}, u32[]{:S(2)}) %collective-permute-start.7) | collective-permute-done | bytes 262176 | tf_op jit(solution)/shard_map/ppermute | solution.py:227
  49.9 0.1 select_select_fusion.8
  50.0 0.9 select_select_fusion.2
  50.9 16.7 %collective-permute-start.10 = (f32[256,256]{1,0:T(8,128)S(1)}, f32[256,256]{1,0:T(8,128)S(1)}, u32[]{:S(2)}, u32[]{:S(2)}) collective-permute-start(f32[256,256]{1,0:T(8,128)S(1)} %select_select_fusion.8), channel_id=1, source_target_pairs={{0,56},{40,48},{8,0},{32,24},{1,57},{41,49},{9,1},{33,25},{2,58},{... | collective-permute-start | bytes 786440 | tf_op jit(solution)/shard_map/ppermute | solution.py:227
  67.6 1.3 collective-permute-start.9
  68.9 0.1 broadcast_bitcast_fusion
  69.0 0.2 mul.190
  69.2 0.8 copy.7
  70.0 0.2 mul.197
  70.2 0.8 copy.9
  71.1 0.2 mul.204
  71.4 0.2 mul.211
  71.6 0.6 collective-permute-done.9
  72.2 0.1 select_select_fusion.7
  72.3 7.0 %collective-permute-start.13 = (f32[512,256]{1,0:T(8,128)S(1)}, f32[512,256]{1,0:T(8,128)S(1)}, u32[]{:S(2)}, u32[]{:S(2)}) collective-permute-start(f32[512,256]{1,0:T(8,128)S(1)} %pad_maximum_fusion.2.mine_ref), channel_id=1, source_target_pairs={{0,1},{1,0},{2,3},{3,2},{4,5},{5,4},{6,7},{7,6},{8,9},{9,8},{10,11... | collective-permute-start | bytes 1572872 | tf_op jit(solution)/shard_map/ppermute | solution.py:267
  79.3 1.0 fusion.3
  80.3 2.0 %collective-permute-start.16 = (bf16[256,512]{1,0:T(8,128)(2,1)}, bf16[256,512]{1,0:T(8,128)(2,1)}, u32[]{:S(2)}, u32[]{:S(2)}) collective-permute-start(bf16[256,512]{1,0:T(8,128)(2,1)} %fusion.3), channel_id=1, source_target_pairs={{0,16},{8,56},{1,17},{9,57},{2,18},{10,58},{3,19},{11,59},{4,20},{... | collective-permute-start | bytes 786440 | tf_op jit(solution)/shard_map/ppermute | solution.py:227
  82.2 2.4 %collective-permute-start.15 = (bf16[256,512]{1,0:T(8,128)(2,1)}, bf16[256,512]{1,0:T(8,128)(2,1)}, u32[]{:S(2)}, u32[]{:S(2)}) collective-permute-start(bf16[256,512]{1,0:T(8,128)(2,1)} %fusion.3), channel_id=1, source_target_pairs={{0,40},{8,32},{1,41},{9,33},{2,42},{10,34},{3,43},{11,35},{4,44},{... | collective-permute-start | bytes 786440 | tf_op jit(solution)/shard_map/ppermute | solution.py:227
  84.6 0.1 reshape.80.place
  84.7 0.1 pad_add_fusion.where
  84.8 0.7 collective-permute-start.12
  85.5 1.9 %collective-permute-start.11 = (bf16[1024,256]{1,0:T(8,128)(2,1)}, bf16[1024,256]{1,0:T(8,128)(2,1)S(1)}, u32[]{:S(2)}, u32[]{:S(2)}) collective-permute-start(bf16[1024,256]{1,0:T(8,128)(2,1)} %select_select_fusion.2), channel_id=1, source_target_pairs={{0,2},{6,64},{66,68},{64,66},{70,0},{2,4},{1,3},{7,65},{67,69},{65... | collective-permute-start | bytes 1572872 | tf_op jit(solution)/shard_map/ppermute | solution.py:227
  87.4 0.3 collective-permute-done.16
  87.8 7.8 %collective-permute-done.15 = bf16[256,512]{1,0:T(8,128)(2,1)} collective-permute-done((bf16[256,512]{1,0:T(8,128)(2,1)}, bf16[256,512]{1,0:T(8,128)(2,1)}, u32[]{:S(2)}, u32[]{:S(2)}) %collective-permute-start.15) | collective-permute-done | bytes 262176 | tf_op jit(solution)/shard_map/ppermute | solution.py:227
  95.5 1.0 select_select_fusion.5
  96.6 10.5 %shard_map.46 = (f32[256,256]{1,0:T(8,128)S(1)}, f32[256,256]{1,0:T(8,128)S(1)}, f32[256,256]{1,0:T(8,128)S(1)}) custom-call(s32[3]{0:T(128)S(1)} %pad_add_fusion.where, f32[512,256]{1,0:T(8,128)S(1)} %pad_maximum_fusion.2.mine_ref, f32[512,256]{1,0:T(8,128)S(1)} %collective-permute-done.13.theirs_ref), custom_call_target="tpu_custom_call" | custom-call | flops 10000000000 | bytes 1048576 | tf_op jit(solution)/shard_map/pallas_call | solution.py:113
  107.1 2.1 %collective-permute-start.18 = (bf16[256,512]{1,0:T(8,128)(2,1)S(1)}, bf16[256,512]{1,0:T(8,128)(2,1)S(1)}, u32[]{:S(2)}, u32[]{:S(2)}) collective-permute-start(bf16[256,512]{1,0:T(8,128)(2,1)S(1)} %select_select_fusion.5), channel_id=1, source_target_pairs={{0,56},{40,48},{8,0},{32,24},{1,57},{41,49},{9,1},{33,25},{2,58},{... | collective-permute-start | bytes 786440 | tf_op jit(solution)/shard_map/ppermute | solution.py:227
  109.1 3.6 %collective-permute-start.17 = (bf16[256,512]{1,0:T(8,128)(2,1)S(1)}, bf16[256,512]{1,0:T(8,128)(2,1)S(1)}, u32[]{:S(2)}, u32[]{:S(2)}) collective-permute-start(bf16[256,512]{1,0:T(8,128)(2,1)S(1)} %select_select_fusion.5), channel_id=1, source_target_pairs={{0,8},{40,32},{16,24},{8,16},{32,40},{56,48},{1,9},{41,33},{17,25}... | collective-permute-start | bytes 786440 | tf_op jit(solution)/shard_map/ppermute | solution.py:227
  112.7 0.1 select_select_fusion.1
  112.8 0.1 fusion.4
  112.9 3.8 %fusion.8 = (f32[256,256]{1,0:T(8,128)S(1)}, f32[256,256]{1,0:T(8,128)S(1)}, f32[256,256]{1,0:T(8,128)S(1)}) fusion(f32[768,256]{1,0:T(8,128)S(1)} %fusion.4, f32[]{:T(128)} %bitcast.9, f32[]{:T(128)} %bitcast.8, bf16[512,256]{1,0:T(8,128)(2,1)S(1)} %copy-done.9, bf16[512,256]{1,0:T(8,128)(2,1)S(1)} %copy-done.7, f32[]{:T(128)} %bitcast.11, f32[]{:T(128)} %bitcast.10, ...), kind=kLoop, calls=%fused_computation.22 | loop fusion | flops 1048576 | bytes 2097176 | tf_op jit(solution)/shard_map/add | solution.py:319
  116.7 0.1 pad_maximum_fusion.mine_ref
  116.8 3.3 %collective-permute-start.14 = (f32[1024,256]{1,0:T(8,128)S(1)}, f32[1024,256]{1,0:T(8,128)S(1)}, u32[]{:S(2)}, u32[]{:S(2)}) collective-permute-start(f32[1024,256]{1,0:T(8,128)S(1)} %pad_maximum_fusion.mine_ref), channel_id=1, source_target_pairs={{0,1},{1,0},{2,3},{3,2},{4,5},{5,4},{6,7},{7,6},{8,9},{9,8},{10,11... | collective-permute-start | bytes 3145736 | tf_op jit(solution)/shard_map/ppermute | solution.py:267
  120.1 8.8 %shard_map.47.x1_ref = f32[256,256]{1,0:T(8,128)S(1)} custom-call(f32[256,256]{1,0:T(8,128)S(1)} %get-tuple-element.27.rest_ref), custom_call_target="tpu_custom_call" | custom-call | flops 10000000000 | bytes 1048576 | tf_op jit(solution)/shard_map/pallas_call | solution.py:124
  128.9 0.1 select_select_fusion.3
  129.0 7.6 %shard_map.48 = f32[1024,512]{1,0:T(8,128)} custom-call(f32[64]{0:T(128)S(1)} %reshape.80.place, s32[3]{0:T(128)S(1)} %pad_add_fusion.where, bf16[1024,512]{1,0:T(8,128)(2,1)S(1)} %bitcast.51, bf16[512,512]{1,0:T(8,128)(2,1)S(1)} %bitcast.54, bf16[512,512]{1,0:T(8,128)(2,1)S(1)} %collective-permute-done.2.sib_ref, f32[1024,256]{1,0:T(8,128)S(1)} %pad_maximum_fusion.mine_ref, ...), custom_call_target="tpu_custom_call" | custom-call | tf_op jit(solution)/shard_map/pallas_call | solution.py:192
  (54 shorter events, 0.4 us)
Async XLA Ops:
  0.0 5.2 %copy-start = (s32[8,16,16]{2,1,0:T(8,128)S(1)}, s32[8,16,16]{2,1,0:T(8,128)}, u32[]{:S(2)}) copy-start(s32[8,16,16]{2,1,0:T(8,128)} %param.7) | copy-start | bytes 24580
  0.0 5.1 %copy-start.10 = (s32[8,16]{1,0:T(8,128)S(1)}, s32[8,16]{1,0:T(8,128)}, u32[]{:S(2)}) copy-start(s32[8,16]{1,0:T(8,128)} %param.6) | copy-start | bytes 1540
  1.0 16.6 %copy-start.2 = (bf16[1,512,512]{2,1,0:T(8,128)(2,1)S(1)}, bf16[1,512,512]{2,1,0:T(8,128)(2,1)}, u32[]{:S(2)}) copy-start(bf16[1,512,512]{2,1,0:T(8,128)(2,1)} %param.5) | copy-start | bytes 1572868
  2.1 12.1 %collective-permute-start.1 = (bf16[512,256]{1,0:T(8,128)(2,1)S(1)}, bf16[512,256]{1,0:T(8,128)(2,1)S(1)}, u32[]{:S(2)}, u32[]{:S(2)}) collective-permute-start(bf16[512,256]{1,0:T(8,128)(2,1)S(1)} %pad_maximum_fusion.3), channel_id=1, source_target_pairs={{0,66},{64,2},{1,67},{65,3},{8,74},{72,10},{9,75},{73,11},{16,82},... | collective-permute-start | bytes 786440 | tf_op jit(solution)/shard_map/ppermute | solution.py:227
  3.4 10.8 %collective-permute-start = (bf16[512,256]{1,0:T(8,128)(2,1)S(1)}, bf16[512,256]{1,0:T(8,128)(2,1)S(1)}, u32[]{:S(2)}, u32[]{:S(2)}) collective-permute-start(bf16[512,256]{1,0:T(8,128)(2,1)S(1)} %pad_maximum_fusion.3), channel_id=1, source_target_pairs={{0,6},{64,70},{1,7},{65,71},{8,14},{72,78},{9,15},{73,79},{16,22},... | collective-permute-start | bytes 786440 | tf_op jit(solution)/shard_map/ppermute | solution.py:227
  14.2 6.1 %collective-permute-start.4 = (bf16[512,256]{1,0:T(8,128)(2,1)S(1)}, bf16[512,256]{1,0:T(8,128)(2,1)S(1)}, u32[]{:S(2)}, u32[]{:S(2)}) collective-permute-start(bf16[512,256]{1,0:T(8,128)(2,1)S(1)} %select_select_fusion.11), channel_id=1, source_target_pairs={{0,70},{6,4},{64,6},{70,68},{1,71},{7,5},{65,7},{71,69},{8,78},{14... | collective-permute-start | bytes 786440 | tf_op jit(solution)/shard_map/ppermute | solution.py:227
  14.9 10.8 %collective-permute-start.3 = (bf16[512,256]{1,0:T(8,128)(2,1)S(1)}, bf16[512,256]{1,0:T(8,128)(2,1)S(1)}, u32[]{:S(2)}, u32[]{:S(2)}) collective-permute-start(bf16[512,256]{1,0:T(8,128)(2,1)S(1)} %select_select_fusion.11), channel_id=1, source_target_pairs={{0,2},{6,64},{66,68},{64,66},{70,0},{2,4},{1,3},{7,65},{67,69},{65... | collective-permute-start | bytes 786440 | tf_op jit(solution)/shard_map/ppermute | solution.py:227
  17.6 32.4 %collective-permute-start.6 = (bf16[1024,256]{1,0:T(8,128)(2,1)S(1)}, bf16[1024,256]{1,0:T(8,128)(2,1)S(1)}, u32[]{:S(2)}, u32[]{:S(2)}) collective-permute-start(bf16[1024,256]{1,0:T(8,128)(2,1)S(1)} %pad_maximum_fusion.1), channel_id=1, source_target_pairs={{0,66},{64,2},{1,67},{65,3},{8,74},{72,10},{9,75},{73,11},{16,82},... | collective-permute-start | bytes 1572872 | tf_op jit(solution)/shard_map/ppermute | solution.py:227
  18.9 31.1 %collective-permute-start.5 = (bf16[1024,256]{1,0:T(8,128)(2,1)S(1)}, bf16[1024,256]{1,0:T(8,128)(2,1)}, u32[]{:S(2)}, u32[]{:S(2)}) collective-permute-start(bf16[1024,256]{1,0:T(8,128)(2,1)S(1)} %pad_maximum_fusion.1), channel_id=1, source_target_pairs={{0,6},{64,70},{1,7},{65,71},{8,14},{72,78},{9,15},{73,79},{16,22},... | collective-permute-start | bytes 1572872 | tf_op jit(solution)/shard_map/ppermute | solution.py:227
  25.7 13.6 %copy-start.6 = (bf16[512,256]{1,0:T(8,128)(2,1)}, bf16[512,256]{1,0:T(8,128)(2,1)S(1)}, u32[]{:S(2)}) copy-start(bf16[512,256]{1,0:T(8,128)(2,1)S(1)} %get-tuple-element.42) | copy-start | bytes 786436
  25.7 13.6 %copy-start.8 = (bf16[512,256]{1,0:T(8,128)(2,1)}, bf16[512,256]{1,0:T(8,128)(2,1)S(1)}, u32[]{:S(2)}) copy-start(bf16[512,256]{1,0:T(8,128)(2,1)S(1)} %get-tuple-element.43) | copy-start | bytes 786436
  27.2 18.7 %collective-permute-start.8 = (f32[256,256]{1,0:T(8,128)S(1)}, f32[256,256]{1,0:T(8,128)S(1)}, u32[]{:S(2)}, u32[]{:S(2)}) collective-permute-start(f32[256,256]{1,0:T(8,128)S(1)} %fusion.6), channel_id=1, source_target_pairs={{0,16},{8,56},{1,17},{9,57},{2,18},{10,58},{3,19},{11,59},{4,20},{... | collective-permute-start | bytes 786440 | tf_op jit(solution)/shard_map/ppermute | solution.py:227
  33.0 16.9 %collective-permute-start.7 = (f32[256,256]{1,0:T(8,128)S(1)}, f32[256,256]{1,0:T(8,128)}, u32[]{:S(2)}, u32[]{:S(2)}) collective-permute-start(f32[256,256]{1,0:T(8,128)S(1)} %fusion.6), channel_id=1, source_target_pairs={{0,40},{8,32},{1,41},{9,33},{2,42},{10,34},{3,43},{11,35},{4,44},{... | collective-permute-start | bytes 786440 | tf_op jit(solution)/shard_map/ppermute | solution.py:227
  39.4 31.7 %collective-permute-start.2 = (bf16[512,512]{1,0:T(8,128)(2,1)S(1)}, bf16[512,512]{1,0:T(8,128)(2,1)S(1)}, u32[]{:S(2)}, u32[]{:S(2)}) collective-permute-start(bf16[512,512]{1,0:T(8,128)(2,1)S(1)} %bitcast.53), channel_id=1, source_target_pairs={{0,64},{64,0},{1,65},{65,1},{2,66},{66,2},{3,67},{67,3},{4,68},{68... | collective-permute-start | bytes 1572872 | tf_op jit(solution)/shard_map/ppermute | solution.py:293
  50.9 20.7 %collective-permute-start.10 = (f32[256,256]{1,0:T(8,128)S(1)}, f32[256,256]{1,0:T(8,128)S(1)}, u32[]{:S(2)}, u32[]{:S(2)}) collective-permute-start(f32[256,256]{1,0:T(8,128)S(1)} %select_select_fusion.8), channel_id=1, source_target_pairs={{0,56},{40,48},{8,0},{32,24},{1,57},{41,49},{9,1},{33,25},{2,58},{... | collective-permute-start | bytes 786440 | tf_op jit(solution)/shard_map/ppermute | solution.py:227
  67.6 4.6 %collective-permute-start.9 = (f32[256,256]{1,0:T(8,128)S(1)}, f32[256,256]{1,0:T(8,128)S(1)}, u32[]{:S(2)}, u32[]{:S(2)}) collective-permute-start(f32[256,256]{1,0:T(8,128)S(1)} %select_select_fusion.8), channel_id=1, source_target_pairs={{0,8},{40,32},{16,24},{8,16},{32,40},{56,48},{1,9},{41,33},{17,25}... | collective-permute-start | bytes 786440 | tf_op jit(solution)/shard_map/ppermute | solution.py:227
  71.3 7.9 %copy-start.1 = (bf16[1,1024,512]{2,1,0:T(8,128)(2,1)S(1)}, bf16[1,1024,512]{2,1,0:T(8,128)(2,1)}, u32[]{:S(2)}) copy-start(bf16[1,1024,512]{2,1,0:T(8,128)(2,1)} %param.4) | copy-start | bytes 3145732
  71.3 7.9 %copy-start.3 = (f32[32,8,2,256]{3,1,2,0:T(8,128)S(1)}, f32[32,8,2,256]{3,1,2,0:T(8,128)}, u32[]{:S(2)}) copy-start(f32[32,8,2,256]{3,1,2,0:T(8,128)} %copy.7) | copy-start | bytes 1572868
  71.3 7.9 %copy-start.4 = (f32[32,8,2,256]{3,1,2,0:T(8,128)S(1)}, f32[32,8,2,256]{3,1,2,0:T(8,128)}, u32[]{:S(2)}) copy-start(f32[32,8,2,256]{3,1,2,0:T(8,128)} %copy.9) | copy-start | bytes 1572868
  72.3 24.3 %collective-permute-start.13 = (f32[512,256]{1,0:T(8,128)S(1)}, f32[512,256]{1,0:T(8,128)S(1)}, u32[]{:S(2)}, u32[]{:S(2)}) collective-permute-start(f32[512,256]{1,0:T(8,128)S(1)} %pad_maximum_fusion.2.mine_ref), channel_id=1, source_target_pairs={{0,1},{1,0},{2,3},{3,2},{4,5},{5,4},{6,7},{7,6},{8,9},{9,8},{10,11... | collective-permute-start | bytes 1572872 | tf_op jit(solution)/shard_map/ppermute | solution.py:267
  80.3 7.5 %collective-permute-start.16 = (bf16[256,512]{1,0:T(8,128)(2,1)}, bf16[256,512]{1,0:T(8,128)(2,1)}, u32[]{:S(2)}, u32[]{:S(2)}) collective-permute-start(bf16[256,512]{1,0:T(8,128)(2,1)} %fusion.3), channel_id=1, source_target_pairs={{0,16},{8,56},{1,17},{9,57},{2,18},{10,58},{3,19},{11,59},{4,20},{... | collective-permute-start | bytes 786440 | tf_op jit(solution)/shard_map/ppermute | solution.py:227
  82.2 13.3 %collective-permute-start.15 = (bf16[256,512]{1,0:T(8,128)(2,1)}, bf16[256,512]{1,0:T(8,128)(2,1)}, u32[]{:S(2)}, u32[]{:S(2)}) collective-permute-start(bf16[256,512]{1,0:T(8,128)(2,1)} %fusion.3), channel_id=1, source_target_pairs={{0,40},{8,32},{1,41},{9,33},{2,42},{10,34},{3,43},{11,35},{4,44},{... | collective-permute-start | bytes 786440 | tf_op jit(solution)/shard_map/ppermute | solution.py:227
  84.8 27.9 %collective-permute-start.12 = (bf16[1024,256]{1,0:T(8,128)(2,1)}, bf16[1024,256]{1,0:T(8,128)(2,1)S(1)}, u32[]{:S(2)}, u32[]{:S(2)}) collective-permute-start(bf16[1024,256]{1,0:T(8,128)(2,1)} %select_select_fusion.2), channel_id=1, source_target_pairs={{0,70},{6,4},{64,6},{70,68},{1,71},{7,5},{65,7},{71,69},{8,78},{14... | collective-permute-start | bytes 1572872 | tf_op jit(solution)/shard_map/ppermute | solution.py:227
  85.5 27.2 %collective-permute-start.11 = (bf16[1024,256]{1,0:T(8,128)(2,1)}, bf16[1024,256]{1,0:T(8,128)(2,1)S(1)}, u32[]{:S(2)}, u32[]{:S(2)}) collective-permute-start(bf16[1024,256]{1,0:T(8,128)(2,1)} %select_select_fusion.2), channel_id=1, source_target_pairs={{0,2},{6,64},{66,68},{64,66},{70,0},{2,4},{1,3},{7,65},{67,69},{65... | collective-permute-start | bytes 1572872 | tf_op jit(solution)/shard_map/ppermute | solution.py:227
  96.5 16.2 %copy-start.5 = (bf16[1024,256]{1,0:T(8,128)(2,1)S(1)}, bf16[1024,256]{1,0:T(8,128)(2,1)}, u32[]{:S(2)}) copy-start(bf16[1024,256]{1,0:T(8,128)(2,1)} %select_select_fusion.2) | copy-start | bytes 1572868
  107.0 5.9 %copy-start.7 = (bf16[512,256]{1,0:T(8,128)(2,1)S(1)}, bf16[512,256]{1,0:T(8,128)(2,1)}, u32[]{:S(2)}) copy-start(bf16[512,256]{1,0:T(8,128)(2,1)} %copy-done.6) | copy-start | bytes 786436
  107.0 5.9 %copy-start.9 = (bf16[512,256]{1,0:T(8,128)(2,1)S(1)}, bf16[512,256]{1,0:T(8,128)(2,1)}, u32[]{:S(2)}) copy-start(bf16[512,256]{1,0:T(8,128)(2,1)} %copy-done.8) | copy-start | bytes 786436
  107.1 21.9 %collective-permute-start.18 = (bf16[256,512]{1,0:T(8,128)(2,1)S(1)}, bf16[256,512]{1,0:T(8,128)(2,1)S(1)}, u32[]{:S(2)}, u32[]{:S(2)}) collective-permute-start(bf16[256,512]{1,0:T(8,128)(2,1)S(1)} %select_select_fusion.5), channel_id=1, source_target_pairs={{0,56},{40,48},{8,0},{32,24},{1,57},{41,49},{9,1},{33,25},{2,58},{... | collective-permute-start | bytes 786440 | tf_op jit(solution)/shard_map/ppermute | solution.py:227
  109.1 19.8 %collective-permute-start.17 = (bf16[256,512]{1,0:T(8,128)(2,1)S(1)}, bf16[256,512]{1,0:T(8,128)(2,1)S(1)}, u32[]{:S(2)}, u32[]{:S(2)}) collective-permute-start(bf16[256,512]{1,0:T(8,128)(2,1)S(1)} %select_select_fusion.5), channel_id=1, source_target_pairs={{0,8},{40,32},{16,24},{8,16},{32,40},{56,48},{1,9},{41,33},{17,25}... | collective-permute-start | bytes 786440 | tf_op jit(solution)/shard_map/ppermute | solution.py:227
  116.8 12.2 %collective-permute-start.14 = (f32[1024,256]{1,0:T(8,128)S(1)}, f32[1024,256]{1,0:T(8,128)S(1)}, u32[]{:S(2)}, u32[]{:S(2)}) collective-permute-start(f32[1024,256]{1,0:T(8,128)S(1)} %pad_maximum_fusion.mine_ref), channel_id=1, source_target_pairs={{0,1},{1,0},{2,3},{3,2},{4,5},{5,4},{6,7},{7,6},{8,9},{9,8},{10,11... | collective-permute-start | bytes 3145736 | tf_op jit(solution)/shard_map/ppermute | solution.py:267

commit v3 on v2

--- a/solution.py
+++ b/solution.py
@@ -88,14 +88,14 @@
     x_ref[H:, 0:H] = corner
 
 
-def first_kernel(where, mine_ref, theirs_ref, x0_ref, l10_ref, rest_ref, work):
+def first_kernel(where, row0_ref, row1_ref, theirs_ref, x0_ref, l10_ref, rest_ref, work):
     even = where[2] == 0
-    work[...] = jnp.where(even, mine_ref[0:B], theirs_ref[0:B])
+    work[...] = jnp.where(even, row0_ref[...], theirs_ref[...])
     store_inverse(x0_ref, factor_tile(work, 0))
-    d01 = jnp.where(even, theirs_ref[0:B], mine_ref[0:B])
-    low = matmul(d01.T, x0_ref[...], NT)
+    d10 = jnp.where(even, row1_ref[...], row0_ref[...].T)
+    low = matmul(d10, x0_ref[...], NT)
     l10_ref[...] = low
-    rest_ref[...] = jnp.where(even, theirs_ref[B:], mine_ref[B:]) - matmul(low, low, NT)
+    rest_ref[...] = jnp.where(even, theirs_ref[...], row1_ref[...]) - matmul(low, low, NT)
 
 
 def second_kernel(rest_ref, x1_ref, work):
@@ -109,15 +109,15 @@
 PARAMS = pltpu.CompilerParams(vmem_limit_bytes=32 * 2**20)
 
 
-def first_pivot(where, mine, theirs):
+def first_pivot(where, row0, row1, theirs):
     return pl.pallas_call(
         first_kernel,
         out_shape=(TILE, TILE, TILE),
-        in_specs=[pl.BlockSpec(memory_space=pltpu.SMEM), VMEM, VMEM],
+        in_specs=[pl.BlockSpec(memory_space=pltpu.SMEM), VMEM, VMEM, VMEM],
         scratch_shapes=[pltpu.VMEM((B, B), F32)],
         compiler_params=PARAMS,
         cost_estimate=COST,
-    )(where, mine, theirs)
+    )(where, row0, row1, theirs)
 
 
 def second_pivot(rest):
@@ -302,17 +302,18 @@
     rest = jnp.concatenate([parent[B:, :B], child[B:, :B]], axis=0)
     rest_held = spread_y.start(tie(rest, held))
     top_held = spread_z.start(top)
-    pivot_rows = jnp.concatenate(spread_z.end(tie(top_held, rest_held)), axis=0)
-    theirs = other(tie(pivot_rows, sibling))
+    row0, row1 = spread_z.end(tie(top_held, rest_held))
+    mine = jnp.where(core == 0, row0, row1)
+    theirs = other(mine)
 
     strip = parent[:B].astype(F32).reshape(B, 2, B)
     for k, ref in ((0, child[:B]), (1, sibling[:B])):
         for b in range(2):
             strip += place[k, 0, b, 0][None, :, None] * ref[:, None, b * B : (b + 1) * B].astype(F32)
-    strip_held = spread_z.start(tie(strip.reshape(B, 2 * B).astype(BF16), pivot_rows))
-    rest0, rest4 = spread_y.end(tie(rest_held, pivot_rows))
-
-    x0, l10, low = first_pivot(where, pivot_rows, theirs)
+    strip_held = spread_z.start(tie(strip.reshape(B, 2 * B).astype(BF16), mine))
+    rest0, rest4 = spread_y.end(tie(rest_held, mine))
+
+    x0, l10, low = first_pivot(tie(where, sibling), row0, row1, theirs)
     g, h = spread_z.end(tie(strip_held, x0))
     tiles = jnp.where(core == 0, rest0[: 3 * B], rest4[: 3 * B]).astype(F32)
     below = [

time: 137 us -> 127 us (0.927)
  the two profiles are of different devices: /device:TPU:11 before, /device:TPU:6 now
where the time goes in v3:
time: 127 us; the launch traced here: 125 us
  starting transfers between devices  69 us (54%)
  Pallas kernels  26.9 us (21%)
  waiting for transfers between devices  12.9 us (10%)
  other arithmetic  9.08 us (7%)
  local copies, waits for them, and re-layouts  6.08 us (5%)
    ppermute x16, starting transfers between devices, send(): return lax.ppermute(value, self.axes, self.routes[k])  59.1 us
    pallas_call x1, Pallas kernels, first_pivot(): pl.pallas_call(first_kernel, out_shape=(TILE, TILE, TILE), in_specs=[pl.B...  10.4 us
    pallas_call x1, Pallas kernels, second_pivot(): pl.pallas_call(second_kernel, out_shape=TILE, in_specs=[VMEM], scratch_sh...  8.8 us
    ppermute x1, waiting for transfers between devices, on_device(): swap = lambda value: lax.ppermute(value, 'y_hi', [(0, 1), (1, 0)])  8.77 us
    pallas_call x1, Pallas kernels, finish(): pl.pallas_call(final_kernel, out_shape=jax.ShapeDtypeStruct(parent.shape,...  7.67 us
    ppermute x1, starting transfers between devices, on_device(): swap = lambda value: lax.ppermute(value, 'y_hi', [(0, 1), (1, 0)])  6.05 us
    ppermute x16, waiting for transfers between devices, send(): return lax.ppermute(value, self.axes, self.routes[k])  4.14 us
    add x1, other arithmetic, on_device(): tiles[(s - 1) * B:s * B]  3.92 us
  transfers between devices with their start and end apart: 19, of which 5 were waited for; matrix products, arithmetic and copies ran while one was open for 9% of the time, Pallas kernels for 15%

profile of v3, /device:TPU:6, one launch (start us, length us, event | category | flops | bytes accessed | tf_op | source)
XLA Modules:
  0.0 124.6 jit_solution(1656343672236716376)
XLA Ops:
  0.0 1.0 fusion.12
  1.0 0.0 copy-start.2
  1.1 1.0 slice.140
  2.1 5.5 %collective-permute-start = (bf16[512,256]{1,0:T(8,128)(2,1)S(1)}, bf16[512,256]{1,0:T(8,128)(2,1)S(1)}, u32[]{:S(2)}, u32[]{:S(2)}) collective-permute-start(bf16[512,256]{1,0:T(8,128)(2,1)S(1)} %pad_maximum_fusion.2), channel_id=1, source_target_pairs={{0,6},{64,70},{1,7},{65,71},{8,14},{72,78},{9,15},{73,79},{16,22},... | collective-permute-start | bytes 786440 | tf_op jit(solution)/shard_map/ppermute | solution.py:227
  7.6 2.1 %collective-permute-start.1 = (bf16[512,256]{1,0:T(8,128)(2,1)S(1)}, bf16[512,256]{1,0:T(8,128)(2,1)S(1)}, u32[]{:S(2)}, u32[]{:S(2)}) collective-permute-start(bf16[512,256]{1,0:T(8,128)(2,1)S(1)} %pad_maximum_fusion.2), channel_id=1, source_target_pairs={{0,66},{64,2},{1,67},{65,3},{8,74},{72,10},{9,75},{73,11},{16,82},... | collective-permute-start | bytes 786440 | tf_op jit(solution)/shard_map/ppermute | solution.py:227
  9.7 1.0 slice.148
  10.8 0.1 reshape.77
  10.9 0.2 compare_reduce_fusion
  11.2 0.2 compare_reduce_fusion.2
  11.4 0.1 reshape.79
  11.4 0.2 dynamic-slice_reduce_fusion.2
  11.7 0.2 compare_reduce_fusion.1
  11.9 0.1 broadcast_compare_fusion
  12.0 0.1 and_convert_fusion.1
  12.0 0.1 and_convert_fusion
  12.2 0.1 broadcast_bitcast_fusion.2
  12.3 0.8 collective-permute-done
  13.1 2.1 %collective-permute-done.1 = bf16[512,256]{1,0:T(8,128)(2,1)S(1)} collective-permute-done((bf16[512,256]{1,0:T(8,128)(2,1)S(1)}, bf16[512,256]{1,0:T(8,128)(2,1)S(1)}, u32[]{:S(2)}, u32[]{:S(2)}) %collective-permute-start.1) | collective-permute-done | bytes 262176 | tf_op jit(solution)/shard_map/ppermute | solution.py:227
  15.2 0.1 select_select_fusion.11
  15.3 5.2 %collective-permute-start.3 = (bf16[512,256]{1,0:T(8,128)(2,1)S(1)}, bf16[512,256]{1,0:T(8,128)(2,1)S(1)}, u32[]{:S(2)}, u32[]{:S(2)}) collective-permute-start(bf16[512,256]{1,0:T(8,128)(2,1)S(1)} %select_select_fusion.11), channel_id=1, source_target_pairs={{0,2},{6,64},{66,68},{64,66},{70,0},{2,4},{1,3},{7,65},{67,69},{65... | collective-permute-start | bytes 786440 | tf_op jit(solution)/shard_map/ppermute | solution.py:227
  20.6 1.8 %collective-permute-start.4 = (bf16[512,256]{1,0:T(8,128)(2,1)S(1)}, bf16[512,256]{1,0:T(8,128)(2,1)S(1)}, u32[]{:S(2)}, u32[]{:S(2)}) collective-permute-start(bf16[512,256]{1,0:T(8,128)(2,1)S(1)} %select_select_fusion.11), channel_id=1, source_target_pairs={{0,70},{6,4},{64,6},{70,68},{1,71},{7,5},{65,7},{71,69},{8,78},{14... | collective-permute-start | bytes 786440 | tf_op jit(solution)/shard_map/ppermute | solution.py:227
  22.4 0.7 fusion.13
  23.1 1.6 %collective-permute-start.5 = (bf16[1024,256]{1,0:T(8,128)(2,1)S(1)}, bf16[1024,256]{1,0:T(8,128)(2,1)S(1)}, u32[]{:S(2)}, u32[]{:S(2)}) collective-permute-start(bf16[1024,256]{1,0:T(8,128)(2,1)S(1)} %pad_maximum_fusion.1), channel_id=1, source_target_pairs={{0,6},{64,70},{1,7},{65,71},{8,14},{72,78},{9,15},{73,79},{16,22},... | collective-permute-start | bytes 1572872 | tf_op jit(solution)/shard_map/ppermute | solution.py:227
  24.7 2.8 %collective-permute-start.6 = (bf16[1024,256]{1,0:T(8,128)(2,1)S(1)}, bf16[1024,256]{1,0:T(8,128)(2,1)}, u32[]{:S(2)}, u32[]{:S(2)}) collective-permute-start(bf16[1024,256]{1,0:T(8,128)(2,1)S(1)} %pad_maximum_fusion.1), channel_id=1, source_target_pairs={{0,66},{64,2},{1,67},{65,3},{8,74},{72,10},{9,75},{73,11},{16,82},... | collective-permute-start | bytes 1572872 | tf_op jit(solution)/shard_map/ppermute | solution.py:227
  27.6 0.0 collective-permute-done.3
  27.6 0.2 collective-permute-done.4
  27.7 0.1 select_select_fusion.10
  27.8 1.3 %fusion.6 = f32[256,256]{1,0:T(8,128)S(1)} fusion(bf16[512,256]{1,0:T(8,128)(2,1)S(1)} %get-tuple-element.44, bf16[512,256]{1,0:T(8,128)(2,1)S(1)} %get-tuple-element.43, f32[]{:T(128)} %bitcast.7, f32[]{:T(128)} %bitcast.6, pred[]{:T(512)S(6)} %eq.183), kind=kLoop, calls=%fused_computation.19 | loop fusion | flops 524288 | bytes 786441 | tf_op jit(solution)/shard_map/add | solution.py:300
  29.1 11.6 %collective-permute-start.7 = (f32[256,256]{1,0:T(8,128)S(1)}, f32[256,256]{1,0:T(8,128)}, u32[]{:S(2)}, u32[]{:S(2)}) collective-permute-start(f32[256,256]{1,0:T(8,128)S(1)} %fusion.6), channel_id=1, source_target_pairs={{0,40},{8,32},{1,41},{9,33},{2,42},{10,34},{3,43},{11,35},{4,44},{... | collective-permute-start | bytes 786440 | tf_op jit(solution)/shard_map/ppermute | solution.py:227
  40.7 2.0 %collective-permute-start.8 = (f32[256,256]{1,0:T(8,128)S(1)}, f32[256,256]{1,0:T(8,128)}, u32[]{:S(2)}, u32[]{:S(2)}) collective-permute-start(f32[256,256]{1,0:T(8,128)S(1)} %fusion.6), channel_id=1, source_target_pairs={{0,16},{8,56},{1,17},{9,57},{2,18},{10,58},{3,19},{11,59},{4,20},{... | collective-permute-start | bytes 786440 | tf_op jit(solution)/shard_map/ppermute | solution.py:227
  42.7 0.1 broadcast_bitcast_fusion
  42.8 6.0 %collective-permute-start.2 = (bf16[512,512]{1,0:T(8,128)(2,1)S(1)}, bf16[512,512]{1,0:T(8,128)(2,1)S(1)}, u32[]{:S(2)}, u32[]{:S(2)}) collective-permute-start(bf16[512,512]{1,0:T(8,128)(2,1)S(1)} %bitcast.53), channel_id=1, source_target_pairs={{0,64},{64,0},{1,65},{65,1},{2,66},{66,2},{3,67},{67,3},{4,68},{68... | collective-permute-start | bytes 1572872 | tf_op jit(solution)/shard_map/ppermute | solution.py:293
  48.9 1.0 collective-permute-done.7
  49.9 0.8 select_select_fusion.8
  50.6 0.8 copy-done.3
  51.4 0.1 select_select_fusion.2
  51.5 8.9 %collective-permute-start.10 = (f32[256,256]{1,0:T(8,128)}, f32[256,256]{1,0:T(8,128)}, u32[]{:S(2)}, u32[]{:S(2)}) collective-permute-start(f32[256,256]{1,0:T(8,128)} %select_select_fusion.8), channel_id=1, source_target_pairs={{0,56},{40,48},{8,0},{32,24},{1,57},{41,49},{9,1},{33,25},{2,58},{... | collective-permute-start | bytes 786440 | tf_op jit(solution)/shard_map/ppermute | solution.py:227
  60.4 2.0 %collective-permute-start.9 = (f32[256,256]{1,0:T(8,128)}, f32[256,256]{1,0:T(8,128)}, u32[]{:S(2)}, u32[]{:S(2)}) collective-permute-start(f32[256,256]{1,0:T(8,128)} %select_select_fusion.8), channel_id=1, source_target_pairs={{0,8},{40,32},{16,24},{8,16},{32,40},{56,48},{1,9},{41,33},{17,25}... | collective-permute-start | bytes 786440 | tf_op jit(solution)/shard_map/ppermute | solution.py:227
  62.4 0.1 pad_add_fusion.where
  62.5 0.1 reshape.80.place
  62.7 0.2 mul.190
  62.9 0.2 mul.197
  63.1 8.8 %collective-permute-done.2.sib_ref = bf16[512,512]{1,0:T(8,128)(2,1)S(1)} collective-permute-done((bf16[512,512]{1,0:T(8,128)(2,1)S(1)}, bf16[512,512]{1,0:T(8,128)(2,1)S(1)}, u32[]{:S(2)}, u32[]{:S(2)}) %collective-permute-start.2) | collective-permute-done | bytes 524320 | tf_op jit(solution)/shard_map/ppermute | solution.py:293
  71.9 0.2 mul.204
  72.1 0.0 copy-start.1
  72.2 0.2 mul.211
  72.4 1.2 broadcast_select_fusion
  73.6 1.9 %collective-permute-start.13 = (f32[256,256]{1,0:T(8,128)S(1)}, f32[256,256]{1,0:T(8,128)S(1)}, u32[]{:S(2)}, u32[]{:S(2)}) collective-permute-start(f32[256,256]{1,0:T(8,128)S(1)} %get-tuple-element.31), channel_id=1, source_target_pairs={{0,1},{1,0},{2,3},{3,2},{4,5},{5,4},{6,7},{7,6},{8,9},{9,8},{10,11... | collective-permute-start | bytes 786440 | tf_op jit(solution)/shard_map/ppermute | solution.py:267
  75.6 0.3 fusion.3
  75.9 1.9 %collective-permute-start.11 = (bf16[1024,256]{1,0:T(8,128)(2,1)S(1)}, bf16[1024,256]{1,0:T(8,128)(2,1)S(1)}, u32[]{:S(2)}, u32[]{:S(2)}) collective-permute-start(bf16[1024,256]{1,0:T(8,128)(2,1)S(1)} %select_select_fusion.2), channel_id=1, source_target_pairs={{0,2},{6,64},{66,68},{64,66},{70,0},{2,4},{1,3},{7,65},{67,69},{65... | collective-permute-start | bytes 1572872 | tf_op jit(solution)/shard_map/ppermute | solution.py:227
  77.8 5.2 %collective-permute-start.12 = (bf16[1024,256]{1,0:T(8,128)(2,1)S(1)}, bf16[1024,256]{1,0:T(8,128)(2,1)S(1)}, u32[]{:S(2)}, u32[]{:S(2)}) collective-permute-start(bf16[1024,256]{1,0:T(8,128)(2,1)S(1)} %select_select_fusion.2), channel_id=1, source_target_pairs={{0,70},{6,4},{64,6},{70,68},{1,71},{7,5},{65,7},{71,69},{8,78},{14... | collective-permute-start | bytes 1572872 | tf_op jit(solution)/shard_map/ppermute | solution.py:227
  83.0 2.2 %collective-permute-start.15 = (bf16[256,512]{1,0:T(8,128)(2,1)S(1)}, bf16[256,512]{1,0:T(8,128)(2,1)S(1)}, u32[]{:S(2)}, u32[]{:S(2)}) collective-permute-start(bf16[256,512]{1,0:T(8,128)(2,1)S(1)} %fusion.3), channel_id=1, source_target_pairs={{0,40},{8,32},{1,41},{9,33},{2,42},{10,34},{3,43},{11,35},{4,44},{... | collective-permute-start | bytes 786440 | tf_op jit(solution)/shard_map/ppermute | solution.py:227
  85.2 1.3 %collective-permute-start.16 = (bf16[256,512]{1,0:T(8,128)(2,1)S(1)}, bf16[256,512]{1,0:T(8,128)(2,1)S(1)}, u32[]{:S(2)}, u32[]{:S(2)}) collective-permute-start(bf16[256,512]{1,0:T(8,128)(2,1)S(1)} %fusion.3), channel_id=1, source_target_pairs={{0,16},{8,56},{1,17},{9,57},{2,18},{10,58},{3,19},{11,59},{4,20},{... | collective-permute-start | bytes 786440 | tf_op jit(solution)/shard_map/ppermute | solution.py:227
  86.6 10.4 %shard_map.46 = (f32[256,256]{1,0:T(8,128)S(1)}, f32[256,256]{1,0:T(8,128)S(1)}, f32[256,256]{1,0:T(8,128)S(1)}) custom-call(s32[3]{0:T(128)S(1)} %pad_add_fusion.where, f32[256,256]{1,0:T(8,128)S(1)} %get-tuple-element.33.row0_ref, f32[256,256]{1,0:T(8,128)S(1)} %get-tuple-element.32.row1_ref, f32[256,256]{1,0:T(8,128)S(1)} %collective-permute-done.13.theirs_ref), custom_call_target="tpu_custom_call" | custom-call | flops 10000000000 | bytes 1048576 | tf_op jit(solution)/shard_map/pallas_call | solution.py:113
  97.1 2.7 %collective-permute-start.17 = (bf16[256,512]{1,0:T(8,128)(2,1)S(1)}, bf16[256,512]{1,0:T(8,128)(2,1)S(1)}, u32[]{:S(2)}, u32[]{:S(2)}) collective-permute-start(bf16[256,512]{1,0:T(8,128)(2,1)S(1)} %select_select_fusion.5), channel_id=1, source_target_pairs={{0,8},{40,32},{16,24},{8,16},{32,40},{56,48},{1,9},{41,33},{17,25}... | collective-permute-start | bytes 786440 | tf_op jit(solution)/shard_map/ppermute | solution.py:227
  99.8 2.1 %collective-permute-start.18 = (bf16[256,512]{1,0:T(8,128)(2,1)S(1)}, bf16[256,512]{1,0:T(8,128)(2,1)S(1)}, u32[]{:S(2)}, u32[]{:S(2)}) collective-permute-start(bf16[256,512]{1,0:T(8,128)(2,1)S(1)} %select_select_fusion.5), channel_id=1, source_target_pairs={{0,56},{40,48},{8,0},{32,24},{1,57},{41,49},{9,1},{33,25},{2,58},{... | collective-permute-start | bytes 786440 | tf_op jit(solution)/shard_map/ppermute | solution.py:227
  102.0 0.1 select_select_fusion.1
  102.1 0.1 fusion.4
  102.1 3.9 %fusion.8 = (f32[256,256]{1,0:T(8,128)S(1)}, f32[256,256]{1,0:T(8,128)S(1)}, f32[256,256]{1,0:T(8,128)S(1)}) fusion(f32[768,256]{1,0:T(8,128)S(1)} %fusion.4, f32[]{:T(128)} %bitcast.9, f32[]{:T(128)} %bitcast.8, bf16[512,256]{1,0:T(8,128)(2,1)S(1)} %get-tuple-element.44, bf16[512,256]{1,0:T(8,128)(2,1)S(1)} %get-tuple-element.43, f32[]{:T(128)} %bitcast.11, ...), kind=kLoop, calls=%fused_computation.21 | loop fusion | flops 1048576 | bytes 2097176 | tf_op jit(solution)/shard_map/add | solution.py:320
  106.1 0.1 pad_maximum_fusion.mine_ref
  106.1 1.9 %collective-permute-start.14 = (f32[1024,256]{1,0:T(8,128)S(1)}, f32[1024,256]{1,0:T(8,128)S(1)}, u32[]{:S(2)}, u32[]{:S(2)}) collective-permute-start(f32[1024,256]{1,0:T(8,128)S(1)} %pad_maximum_fusion.mine_ref), channel_id=1, source_target_pairs={{0,1},{1,0},{2,3},{3,2},{4,5},{5,4},{6,7},{7,6},{8,9},{9,8},{10,11... | collective-permute-start | bytes 3145736 | tf_op jit(solution)/shard_map/ppermute | solution.py:267
  108.1 8.8 %shard_map.47.x1_ref = f32[256,256]{1,0:T(8,128)S(1)} custom-call(f32[256,256]{1,0:T(8,128)S(1)} %get-tuple-element.27.rest_ref), custom_call_target="tpu_custom_call" | custom-call | flops 10000000000 | bytes 1048576 | tf_op jit(solution)/shard_map/pallas_call | solution.py:124
  116.9 0.1 select_select_fusion.3
  117.0 7.7 %shard_map.48 = f32[1024,512]{1,0:T(8,128)} custom-call(f32[64]{0:T(128)S(1)} %reshape.80.place, s32[3]{0:T(128)S(1)} %pad_add_fusion.where, bf16[1024,512]{1,0:T(8,128)(2,1)S(1)} %bitcast.51, bf16[512,512]{1,0:T(8,128)(2,1)S(1)} %bitcast.54, bf16[512,512]{1,0:T(8,128)(2,1)S(1)} %collective-permute-done.2.sib_ref, f32[1024,256]{1,0:T(8,128)S(1)} %pad_maximum_fusion.mine_ref, ...), custom_call_target="tpu_custom_call" | custom-call | tf_op jit(solution)/shard_map/pallas_call | solution.py:192
  (41 shorter events, 0.4 us)
Async XLA Ops:
  0.0 10.9 %copy-start = (s32[8,16,16]{2,1,0:T(8,128)S(1)}, s32[8,16,16]{2,1,0:T(8,128)}, u32[]{:S(2)}) copy-start(s32[8,16,16]{2,1,0:T(8,128)} %param.7) | copy-start | bytes 24580
  0.0 10.8 %copy-start.4 = (s32[8,16]{1,0:T(8,128)S(1)}, s32[8,16]{1,0:T(8,128)}, u32[]{:S(2)}) copy-start(s32[8,16]{1,0:T(8,128)} %param.6) | copy-start | bytes 1540
  1.0 22.1 %copy-start.2 = (bf16[1,512,512]{2,1,0:T(8,128)(2,1)S(1)}, bf16[1,512,512]{2,1,0:T(8,128)(2,1)}, u32[]{:S(2)}) copy-start(bf16[1,512,512]{2,1,0:T(8,128)(2,1)} %param.5) | copy-start | bytes 1572868
  2.1 11.1 %collective-permute-start = (bf16[512,256]{1,0:T(8,128)(2,1)S(1)}, bf16[512,256]{1,0:T(8,128)(2,1)S(1)}, u32[]{:S(2)}, u32[]{:S(2)}) collective-permute-start(bf16[512,256]{1,0:T(8,128)(2,1)S(1)} %pad_maximum_fusion.2), channel_id=1, source_target_pairs={{0,6},{64,70},{1,7},{65,71},{8,14},{72,78},{9,15},{73,79},{16,22},... | collective-permute-start | bytes 786440 | tf_op jit(solution)/shard_map/ppermute | solution.py:227
  7.6 7.7 %collective-permute-start.1 = (bf16[512,256]{1,0:T(8,128)(2,1)S(1)}, bf16[512,256]{1,0:T(8,128)(2,1)S(1)}, u32[]{:S(2)}, u32[]{:S(2)}) collective-permute-start(bf16[512,256]{1,0:T(8,128)(2,1)S(1)} %pad_maximum_fusion.2), channel_id=1, source_target_pairs={{0,66},{64,2},{1,67},{65,3},{8,74},{72,10},{9,75},{73,11},{16,82},... | collective-permute-start | bytes 786440 | tf_op jit(solution)/shard_map/ppermute | solution.py:227
  15.3 12.2 %collective-permute-start.3 = (bf16[512,256]{1,0:T(8,128)(2,1)S(1)}, bf16[512,256]{1,0:T(8,128)(2,1)S(1)}, u32[]{:S(2)}, u32[]{:S(2)}) collective-permute-start(bf16[512,256]{1,0:T(8,128)(2,1)S(1)} %select_select_fusion.11), channel_id=1, source_target_pairs={{0,2},{6,64},{66,68},{64,66},{70,0},{2,4},{1,3},{7,65},{67,69},{65... | collective-permute-start | bytes 786440 | tf_op jit(solution)/shard_map/ppermute | solution.py:227
  20.6 7.1 %collective-permute-start.4 = (bf16[512,256]{1,0:T(8,128)(2,1)S(1)}, bf16[512,256]{1,0:T(8,128)(2,1)S(1)}, u32[]{:S(2)}, u32[]{:S(2)}) collective-permute-start(bf16[512,256]{1,0:T(8,128)(2,1)S(1)} %select_select_fusion.11), channel_id=1, source_target_pairs={{0,70},{6,4},{64,6},{70,68},{1,71},{7,5},{65,7},{71,69},{8,78},{14... | collective-permute-start | bytes 786440 | tf_op jit(solution)/shard_map/ppermute | solution.py:227
  23.1 27.5 %collective-permute-start.5 = (bf16[1024,256]{1,0:T(8,128)(2,1)S(1)}, bf16[1024,256]{1,0:T(8,128)(2,1)S(1)}, u32[]{:S(2)}, u32[]{:S(2)}) collective-permute-start(bf16[1024,256]{1,0:T(8,128)(2,1)S(1)} %pad_maximum_fusion.1), channel_id=1, source_target_pairs={{0,6},{64,70},{1,7},{65,71},{8,14},{72,78},{9,15},{73,79},{16,22},... | collective-permute-start | bytes 1572872 | tf_op jit(solution)/shard_map/ppermute | solution.py:227
  24.7 26.7 %collective-permute-start.6 = (bf16[1024,256]{1,0:T(8,128)(2,1)S(1)}, bf16[1024,256]{1,0:T(8,128)(2,1)}, u32[]{:S(2)}, u32[]{:S(2)}) collective-permute-start(bf16[1024,256]{1,0:T(8,128)(2,1)S(1)} %pad_maximum_fusion.1), channel_id=1, source_target_pairs={{0,66},{64,2},{1,67},{65,3},{8,74},{72,10},{9,75},{73,11},{16,82},... | collective-permute-start | bytes 1572872 | tf_op jit(solution)/shard_map/ppermute | solution.py:227
  29.1 20.8 %collective-permute-start.7 = (f32[256,256]{1,0:T(8,128)S(1)}, f32[256,256]{1,0:T(8,128)}, u32[]{:S(2)}, u32[]{:S(2)}) collective-permute-start(f32[256,256]{1,0:T(8,128)S(1)} %fusion.6), channel_id=1, source_target_pairs={{0,40},{8,32},{1,41},{9,33},{2,42},{10,34},{3,43},{11,35},{4,44},{... | collective-permute-start | bytes 786440 | tf_op jit(solution)/shard_map/ppermute | solution.py:227
  40.7 9.2 %collective-permute-start.8 = (f32[256,256]{1,0:T(8,128)S(1)}, f32[256,256]{1,0:T(8,128)}, u32[]{:S(2)}, u32[]{:S(2)}) collective-permute-start(f32[256,256]{1,0:T(8,128)S(1)} %fusion.6), channel_id=1, source_target_pairs={{0,16},{8,56},{1,17},{9,57},{2,18},{10,58},{3,19},{11,59},{4,20},{... | collective-permute-start | bytes 786440 | tf_op jit(solution)/shard_map/ppermute | solution.py:227
  42.8 29.1 %collective-permute-start.2 = (bf16[512,512]{1,0:T(8,128)(2,1)S(1)}, bf16[512,512]{1,0:T(8,128)(2,1)S(1)}, u32[]{:S(2)}, u32[]{:S(2)}) collective-permute-start(bf16[512,512]{1,0:T(8,128)(2,1)S(1)} %bitcast.53), channel_id=1, source_target_pairs={{0,64},{64,0},{1,65},{65,1},{2,66},{66,2},{3,67},{67,3},{4,68},{68... | collective-permute-start | bytes 1572872 | tf_op jit(solution)/shard_map/ppermute | solution.py:293
  50.6 0.8 copy-start.3
  51.5 20.9 %collective-permute-start.10 = (f32[256,256]{1,0:T(8,128)}, f32[256,256]{1,0:T(8,128)}, u32[]{:S(2)}, u32[]{:S(2)}) collective-permute-start(f32[256,256]{1,0:T(8,128)} %select_select_fusion.8), channel_id=1, source_target_pairs={{0,56},{40,48},{8,0},{32,24},{1,57},{41,49},{9,1},{33,25},{2,58},{... | collective-permute-start | bytes 786440 | tf_op jit(solution)/shard_map/ppermute | solution.py:227
  60.4 12.0 %collective-permute-start.9 = (f32[256,256]{1,0:T(8,128)}, f32[256,256]{1,0:T(8,128)}, u32[]{:S(2)}, u32[]{:S(2)}) collective-permute-start(f32[256,256]{1,0:T(8,128)} %select_select_fusion.8), channel_id=1, source_target_pairs={{0,8},{40,32},{16,24},{8,16},{32,40},{56,48},{1,9},{41,33},{17,25}... | collective-permute-start | bytes 786440 | tf_op jit(solution)/shard_map/ppermute | solution.py:227
  72.1 3.4 %copy-start.1 = (bf16[1,1024,512]{2,1,0:T(8,128)(2,1)S(1)}, bf16[1,1024,512]{2,1,0:T(8,128)(2,1)}, u32[]{:S(2)}) copy-start(bf16[1,1024,512]{2,1,0:T(8,128)(2,1)} %param.4) | copy-start | bytes 3145732
  73.6 12.9 %collective-permute-start.13 = (f32[256,256]{1,0:T(8,128)S(1)}, f32[256,256]{1,0:T(8,128)S(1)}, u32[]{:S(2)}, u32[]{:S(2)}) collective-permute-start(f32[256,256]{1,0:T(8,128)S(1)} %get-tuple-element.31), channel_id=1, source_target_pairs={{0,1},{1,0},{2,3},{3,2},{4,5},{5,4},{6,7},{7,6},{8,9},{9,8},{10,11... | collective-permute-start | bytes 786440 | tf_op jit(solution)/shard_map/ppermute | solution.py:267
  75.9 26.1 %collective-permute-start.11 = (bf16[1024,256]{1,0:T(8,128)(2,1)S(1)}, bf16[1024,256]{1,0:T(8,128)(2,1)S(1)}, u32[]{:S(2)}, u32[]{:S(2)}) collective-permute-start(bf16[1024,256]{1,0:T(8,128)(2,1)S(1)} %select_select_fusion.2), channel_id=1, source_target_pairs={{0,2},{6,64},{66,68},{64,66},{70,0},{2,4},{1,3},{7,65},{67,69},{65... | collective-permute-start | bytes 1572872 | tf_op jit(solution)/shard_map/ppermute | solution.py:227
  77.8 24.2 %collective-permute-start.12 = (bf16[1024,256]{1,0:T(8,128)(2,1)S(1)}, bf16[1024,256]{1,0:T(8,128)(2,1)S(1)}, u32[]{:S(2)}, u32[]{:S(2)}) collective-permute-start(bf16[1024,256]{1,0:T(8,128)(2,1)S(1)} %select_select_fusion.2), channel_id=1, source_target_pairs={{0,70},{6,4},{64,6},{70,68},{1,71},{7,5},{65,7},{71,69},{8,78},{14... | collective-permute-start | bytes 1572872 | tf_op jit(solution)/shard_map/ppermute | solution.py:227
  83.0 14.0 %collective-permute-start.15 = (bf16[256,512]{1,0:T(8,128)(2,1)S(1)}, bf16[256,512]{1,0:T(8,128)(2,1)S(1)}, u32[]{:S(2)}, u32[]{:S(2)}) collective-permute-start(bf16[256,512]{1,0:T(8,128)(2,1)S(1)} %fusion.3), channel_id=1, source_target_pairs={{0,40},{8,32},{1,41},{9,33},{2,42},{10,34},{3,43},{11,35},{4,44},{... | collective-permute-start | bytes 786440 | tf_op jit(solution)/shard_map/ppermute | solution.py:227
  85.2 11.8 %collective-permute-start.16 = (bf16[256,512]{1,0:T(8,128)(2,1)S(1)}, bf16[256,512]{1,0:T(8,128)(2,1)S(1)}, u32[]{:S(2)}, u32[]{:S(2)}) collective-permute-start(bf16[256,512]{1,0:T(8,128)(2,1)S(1)} %fusion.3), channel_id=1, source_target_pairs={{0,16},{8,56},{1,17},{9,57},{2,18},{10,58},{3,19},{11,59},{4,20},{... | collective-permute-start | bytes 786440 | tf_op jit(solution)/shard_map/ppermute | solution.py:227
  97.1 19.8 %collective-permute-start.17 = (bf16[256,512]{1,0:T(8,128)(2,1)S(1)}, bf16[256,512]{1,0:T(8,128)(2,1)S(1)}, u32[]{:S(2)}, u32[]{:S(2)}) collective-permute-start(bf16[256,512]{1,0:T(8,128)(2,1)S(1)} %select_select_fusion.5), channel_id=1, source_target_pairs={{0,8},{40,32},{16,24},{8,16},{32,40},{56,48},{1,9},{41,33},{17,25}... | collective-permute-start | bytes 786440 | tf_op jit(solution)/shard_map/ppermute | solution.py:227
  99.8 17.1 %collective-permute-start.18 = (bf16[256,512]{1,0:T(8,128)(2,1)S(1)}, bf16[256,512]{1,0:T(8,128)(2,1)S(1)}, u32[]{:S(2)}, u32[]{:S(2)}) collective-permute-start(bf16[256,512]{1,0:T(8,128)(2,1)S(1)} %select_select_fusion.5), channel_id=1, source_target_pairs={{0,56},{40,48},{8,0},{32,24},{1,57},{41,49},{9,1},{33,25},{2,58},{... | collective-permute-start | bytes 786440 | tf_op jit(solution)/shard_map/ppermute | solution.py:227
  106.1 10.8 %collective-permute-start.14 = (f32[1024,256]{1,0:T(8,128)S(1)}, f32[1024,256]{1,0:T(8,128)S(1)}, u32[]{:S(2)}, u32[]{:S(2)}) collective-permute-start(f32[1024,256]{1,0:T(8,128)S(1)} %pad_maximum_fusion.mine_ref), channel_id=1, source_target_pairs={{0,1},{1,0},{2,3},{3,2},{4,5},{5,4},{6,7},{7,6},{8,9},{9,8},{10,11... | collective-permute-start | bytes 3145736 | tf_op jit(solution)/shard_map/ppermute | solution.py:267
